TPU v7x, 32 devices: a whole 2x2x4 slice. The times are simulated.
32 devices in a mesh: expert: 8 (over y, x, core), chan: 4 (over z).
Axes of the slice: x: 2, y: 2, z: 4, core: 2. Of those that a mesh axis runs over, the one named last changes fastest.
Arguments:
- tiles_in: bfloat16 [64, 3, 3, 2048], P('expert', None, None, 'chan'), may hold values from -6 to 6
- grad_out: bfloat16 [64, 3, 3, 2048], P('expert', None, None, 'chan'), may hold values from -6 to 6
- gate: bfloat16 [64], P('expert'), may hold values from 0.19921875 to 1
- expert_id: int32 [64, 1], P('expert'), may hold values from 0 to 7; in each aligned block of 8 rows (0 to 7, 8 to 15, ...) at most 2 rows name the same one
- w_conv: bfloat16 [8, 3, 3, 32, 16384], P('expert', None, None, None, 'chan'), may hold values from -0.375 to 0.375
- w_depth: bfloat16 [8, 9, 16384], P('expert', None, 'chan'), may hold values from -2 to 2
- w_out: bfloat16 [8, 16384, 2048], P('expert', 'chan'), may hold values from -0.046875 to 0.046875
Outputs:
- grad_input: bfloat16 [64, 3, 3, 2048], P('expert', None, None, 'chan')
- grad_gate: bfloat16 [64], P('expert')
Inputs may be any that keep to these rules, and one draw needn't show every extreme that they name: `expert_id`: within the 8 tiles of one index of expert, no expert is named more than 2 times, and in every draw some expert is named exactly 2 times there.
All inputs are finite; a program needn't handle non-finite values.
Results may differ from a plain program's by a relative error of at most 0.009.
Values may be sent and summed in bfloat16 or wider, within the bound.
A program may use at most 64 MiB of HBM per device.

v0:
```python
import jax
import jax.numpy as jnp
from jax import lax
from jax.sharding import PartitionSpec as P

CAP = 2


def group_conv(field, kernel, count):
    return lax.conv_general_dilated(
        field,
        kernel,
        (1, 1),
        "SAME",
        dimension_numbers=("NHWC", "HWIO", "NHWC"),
        feature_group_count=count,
        preferred_element_type=jnp.float32,
    )


def conv_back(field, kernel, count, cotangent):
    forward_value, pullback = jax.vjp(lambda value: group_conv(value, kernel, count), field)
    return pullback(cotangent)[0]


def gelu_slope(value):
    normal_cdf = 0.5 * (1.0 + jax.scipy.special.erf(value * 0.7071067811865476))
    return normal_cdf + value * jnp.exp(-0.5 * value * value) * 0.3989422804014327


def depth_forward(field, taps):
    side = field.shape[1]
    padded = jnp.pad(field, ((0, 0), (1, 1), (1, 1), (0, 0))).astype(jnp.float32)
    total = jnp.zeros(field.shape, jnp.float32)
    for row_off in range(3):
        for col_off in range(3):
            total = total + padded[:, row_off : row_off + side, col_off : col_off + side, :] * taps[
                3 * row_off + col_off
            ].astype(jnp.float32)
    return total


def depth_back(field, taps):
    side = field.shape[1]
    padded = jnp.pad(field, ((0, 0), (1, 1), (1, 1), (0, 0))).astype(jnp.float32)
    total = jnp.zeros(field.shape, jnp.float32)
    for row_off in range(3):
        for col_off in range(3):
            total = total + padded[
                :, 2 - row_off : 2 - row_off + side, 2 - col_off : 2 - col_off + side, :
            ] * taps[3 * row_off + col_off].astype(jnp.float32)
    return total


def on_device(tiles_in, grad_out, gate, expert_id, w_conv, w_depth, w_out):
    owned, side = (tiles_in.shape[0], tiles_in.shape[1])
    local_feat = tiles_in.shape[3]
    sections = lax.axis_size("expert")
    capacity = CAP
    slots = sections * capacity
    chosen = expert_id[:, 0]
    matches = (chosen[:, None] == jnp.arange(sections, dtype=jnp.int32)[None, :]).astype(jnp.int32)
    rows_idx = jnp.arange(owned, dtype=jnp.int32)
    earlier = (rows_idx[:, None] > rows_idx[None, :]).astype(jnp.int32)
    before = jnp.dot(earlier, matches)
    rank = jnp.sum(before * matches, axis=1)
    slot = chosen * capacity + rank
    placing = (slot[:, None] == jnp.arange(slots, dtype=jnp.int32)[None, :]).astype(jnp.bfloat16)
    flat = jnp.concatenate([tiles_in.reshape(owned, -1), grad_out.reshape(owned, -1)], axis=1)
    outward = lax.dot_general(
        placing, flat, (((0,), (0,)), ((), ())), preferred_element_type=jnp.float32
    ).astype(jnp.bfloat16)
    gate_out = lax.dot_general(
        placing,
        gate.reshape(owned, 1),
        (((0,), (0,)), ((), ())),
        preferred_element_type=jnp.float32,
    ).astype(jnp.bfloat16)
    arrived, gate_in = (
        lax.all_to_all(
            outward.reshape(sections, capacity, -1),
            "expert",
            split_axis=0,
            concat_axis=0,
            tiled=True,
        ),
        lax.all_to_all(
            gate_out.reshape(sections, capacity), "expert", split_axis=0, concat_axis=0, tiled=True
        ),
    )
    width = side * side * local_feat
    arrived = arrived.reshape(slots, 2 * width)
    inputs = arrived[:, :width].reshape(slots, side, side, local_feat)
    grads = arrived[:, width:].reshape(slots, side, side, local_feat)
    gates = gate_in.reshape(slots).astype(jnp.float32)
    kernel = w_conv[0]
    taps = w_depth[0]
    project = w_out[0]
    hidden = project.shape[0]
    count = local_feat // kernel.shape[2]
    h_one = group_conv(inputs, kernel, count)
    active = jax.nn.gelu(h_one, approximate=False).astype(jnp.bfloat16)
    h_two = depth_forward(active, taps).astype(jnp.bfloat16)
    gathered = lax.all_gather(grads, "chan", axis=3, tiled=True)
    upper = lax.dot_general(
        gathered.reshape(slots * side * side, -1),
        project,
        (((1,), (1,)), ((), ())),
        preferred_element_type=jnp.float32,
    )
    upper = upper.reshape(slots, side, side, hidden)
    partial_grad = jnp.sum(h_two.astype(jnp.float32) * upper, axis=(1, 2, 3))
    gate_grad = lax.psum(partial_grad, "chan").astype(jnp.bfloat16)
    d_two = (gates[:, None, None, None] * upper).astype(jnp.bfloat16)
    d_act = depth_back(d_two, taps)
    d_one = (d_act * gelu_slope(h_one)).astype(jnp.bfloat16)
    d_input = conv_back(inputs, kernel, count, d_one.astype(jnp.float32))
    back_rows, back_gate = (
        lax.all_to_all(
            d_input.reshape(sections, capacity, -1),
            "expert",
            split_axis=0,
            concat_axis=0,
            tiled=True,
        ),
        lax.all_to_all(
            gate_grad.reshape(sections, capacity), "expert", split_axis=0, concat_axis=0, tiled=True
        ),
    )
    grad_input = jnp.dot(
        placing, back_rows.reshape(slots, -1), preferred_element_type=jnp.float32
    ).astype(jnp.bfloat16)
    grad_gate = jnp.dot(
        placing, back_gate.reshape(slots, 1), preferred_element_type=jnp.float32
    ).astype(jnp.bfloat16)
    return (grad_input.reshape(owned, side, side, local_feat), grad_gate.reshape(owned))


def solution(mesh):
    in_specs = (
        P("expert", None, None, "chan"),
        P("expert", None, None, "chan"),
        P("expert"),
        P("expert", None),
        P("expert", None, None, None, "chan"),
        P("expert", None, "chan"),
        P("expert", "chan", None),
    )
    out_specs = (P("expert", None, None, "chan"), P("expert"))
    return jax.shard_map(
        on_device, mesh=mesh, in_specs=in_specs, out_specs=out_specs, check_vma=False
    )
```

profile of v0, /device:TPU:0, one launch (start us, length us, event | category | flops | bytes accessed | tf_op | source)
XLA Modules:
  0.0 106.6 jit_solution(17537001903222350584)
XLA Ops:
  0.6 0.0 copy-start
  0.6 0.9 fusion.42
  1.5 0.7 fusion.54
  2.2 0.0 copy-done
  2.2 0.2 fusion.44
  2.4 0.7 all_to_all.24
  3.0 5.2 %all-to-all-start = ((bf16[8,1,2]{2,1,0:T(2,128)(2,1)}), bf16[8,1,2]{2,1,0:T(2,128)(2,1)S(1)}, u32[]{:S(2)}, u32[]{:S(2)}) async-start(bf16[8,1,2]{2,1,0:T(2,128)(2,1)} %all_to_all.24), calls=%async_computation | async-start | bytes 8192 | tf_op jit(solution)/shard_map/all_to_all | solution.py:87
  8.2 1.3 %convolution_convert_fusion = bf16[16,9216]{1,0:T(8,128)(2,1)S(1)} fusion(bf16[8,4608]{1,0:T(8,128)(2,1)} %bitcast.87, bf16[8,4608]{1,0:T(8,128)(2,1)} %bitcast.88, s32[8]{0:T(128)S(1)} %fusion.54), kind=kOutput, calls=%fused_computation.2 | convolution fusion | flops 2801792 | bytes 442400 | tf_op jit(solution)/shard_map/dot_general | solution.py:70
  9.5 0.8 reshape.166
  10.3 2.5 %all-to-all-done = bf16[8,1,2]{2,1,0:T(2,128)(2,1)S(1)} async-done(((bf16[8,1,2]{2,1,0:T(2,128)(2,1)}), bf16[8,1,2]{2,1,0:T(2,128)(2,1)S(1)}, u32[]{:S(2)}, u32[]{:S(2)}) %all-to-all-start) | async-done | bytes 64 | tf_op jit(solution)/shard_map/all_to_all | solution.py:87
  12.8 3.4 %all-to-all-start.1 = ((bf16[8,2,9216]{2,1,0:T(2,128)(2,1)}), bf16[8,2,9216]{2,1,0:T(2,128)(2,1)S(1)}, u32[]{:S(2)}, u32[]{:S(2)}) async-start(bf16[8,2,9216]{2,1,0:T(2,128)(2,1)} %reshape.166), calls=%async_computation.1 | async-start | bytes 589824 | tf_op jit(solution)/shard_map/all_to_all | solution.py:80
  16.2 2.0 %slice_convert_fusion.8 = (f32[1,1,4096]{2,1,0:T(1,128)}, f32[1,1,4096]{2,1,0:T(1,128)}, f32[1,1,4096]{2,1,0:T(1,128)}, f32[1,1,4096]{2,1,0:T(1,128)}, f32[1,1,4...) fusion(bf16[1,9,4096]{2,1,0:T(8,128)(2,1)} %param.12), kind=kLoop, calls=%fused_computation.93 | loop fusion | flops 36864 | bytes 221184 | tf_op jit(solution)/shard_map/convert_element_type | solution.py:51
  18.3 2.4 %copy.36 = bf16[36,8,16,256]{3,2,1,0:T(8,128)(2,1)S(1)} copy(bf16[36,8,16,256]{3,1,2,0:T(8,128)(2,1)} %bitcast.67) | data formatting | bytes 4718592
  20.7 2.4 %copy.29 = bf16[3,3,16,32,256]{4,3,2,1,0:T(8,128)(2,1)} copy(bf16[3,3,16,32,256]{4,2,3,1,0:T(8,128)(2,1)S(1)} %bitcast.61) | data formatting | bytes 4718592 | tf_op jit(solution)/shard_map/transpose(jvp())/reshape | solution.py:10
  23.0 3.3 %rev.3 = bf16[3,3,512,256]{3,2,1,0:T(8,128)(2,1)} reverse(bf16[3,3,512,256]{3,2,1,0:T(8,128)(2,1)} %bitcast.65), dimensions={0,1} | reverse | bytes 4718592 | tf_op jit(solution)/shard_map/transpose(jvp())/rev | solution.py:10
  26.3 0.1 reshape.175
  26.4 0.0 all-to-all-done.1
  26.4 0.1 reshape.167
  26.6 0.1 reshape.168
  26.7 17.8 %all_gather.3 = bf16[16,3,3,2048]{3,0,2,1:T(8,128)(2,1)} all-gather(bf16[16,3,3,512]{3,0,2,1:T(8,128)(2,1)S(1)} %copy.25), channel_id=1, replica_groups=mesh['expert'=8,'chan'=4] {'chan'}, dimensions={3}, use_global_device_ids=true | all-gather | bytes 737280 | tf_op jit(solution)/shard_map/all_gather | solution.py:104
  44.5 0.3 reshape.169
  44.9 1.2 %fusion.37 = f32[3,3,16,2,8,256]{5,4,3,2,1,0:T(8,128)S(1)} fusion(bf16[3,3,32,16,256]{4,3,2,1,0:T(8,128)(2,1)S(1)} %bitcast.62, bf16[16,3,3,16,32]{4,3,2,1,0:T(8,128)(2,1)S(1)} %reshape.169), kind=kOutput, calls=%fused_computation.71 | convolution fusion | flops 205520896 | bytes 4866048 | tf_op jit(solution)/shard_map/conv_general_dilated | solution.py:10
  46.0 1.7 %copy.35 = f32[3,3,16,2,8,256]{5,4,2,3,1,0:T(8,128)} copy(f32[3,3,16,2,8,256]{5,4,3,2,1,0:T(8,128)S(1)} %fusion.37) | data formatting | bytes 4718592 | tf_op jit(solution)/shard_map/conv_general_dilated | solution.py:10
  47.7 9.3 %multiply_convert_fusion = (bf16[16,3,3,4096]{3,0,2,1:T(8,128)(2,1)S(1)}, f32[16,3,3,4096]{3,0,2,1:T(8,128)S(1)}) fusion(f32[16]{0:T(128)S(1)} %reshape.175, bf16[16,3,3,2048]{3,0,2,1:T(8,128)(2,1)} %all_gather.3, bf16[1,4096,2048]{2,1,0:T(8,128)(2,1)} %param.13), kind=kOutput, calls=%fused_computation.68 | convolution fusion | flops 2417098752 | bytes 20906048 | tf_op jit(solution)/shard_map/dot_general | solution.py:105
  57.0 0.0 copy-start.2
  57.1 0.0 copy-start.3
  57.1 0.0 copy-start.5
  57.1 0.0 copy-start.7
  57.1 0.0 copy-start.9
  57.1 0.0 copy-start.11
  57.1 0.0 copy-start.13
  57.1 0.0 copy-start.15
  57.1 0.0 copy-start.17
  57.1 0.0 copy-start.19
  57.1 0.7 pad_convert_fusion.1
  57.9 0.8 copy-done.2
  58.7 0.0 copy-done.3
  58.7 0.0 copy-done.5
  58.7 0.0 copy-done.7
  58.7 0.0 copy-done.9
  58.7 0.0 copy-done.11
  58.7 0.0 copy-done.13
  58.7 0.0 copy-done.15
  58.8 0.0 copy-done.17
  58.8 0.0 copy-done.19
  58.8 0.0 copy-start.1
  58.8 7.6 %fusion.10 = (bf16[16,3,3,4096]{3,0,2,1:T(8,128)(2,1)S(1)}, bf16[16,3,3,4096]{3,0,2,1:T(8,128)(2,1)S(1)}) fusion(f32[16,3,3,4096]{3,0,2,1:T(8,128)S(1)} %bitcast.66, f32[4096]{0:T(1024)S(1)} %bitcast.82, f32[16,5,5,4096]{3,0,2,1:T(8,128)S(1)} %pad_convert_fusion.1, f32[4096]{0:T(1024)S(1)} %bitcast.84, f32[4096]{0:T(1024)S(1)} %bitcast.70, ...), kind=kLoop, calls=%fused_computation.16 | loop fusion | flops 54263808 | bytes 26099712 | tf_op jit(solution)/shard_map/convert_element_type | solution.py:102
  66.3 0.0 copy-done.1
  66.4 2.9 %convolution_convert_fusion.2 = bf16[16,3,3,16,32]{4,0,3,2,1:T(8,128)(2,1)S(1)} fusion(bf16[3,3,16,32,256]{4,3,2,1,0:T(8,128)(2,1)S(1)} %bitcast.64, bf16[3,3,2,16,8,256]{5,4,3,2,1,0:T(8,128)(2,1)S(1)} %bitcast.63), kind=kOutput, calls=%fused_computation.72 | convolution fusion | flops 205594624 | bytes 3686400 | tf_op jit(solution)/shard_map/transpose(jvp())/conv_general_dilated | solution.py:10
  69.2 1.0 copy.31
  70.2 2.2 %convert_element_type.194 = bf16[8,2,4608]{2,1,0:T(2,128)(2,1)} reshape(bf16[16,3,3,16,32]{4,3,2,1,0:T(8,128)(2,1)} %copy.31) | data formatting | bytes 294912 | tf_op jit(solution)/shard_map/transpose(jvp())/convert_element_type | solution.py:10
  72.4 0.0 copy-start.12
  72.4 0.0 copy-start.14
  72.4 0.7 pad_convert_fusion
  73.2 2.9 %multiply_reduce_fusion = f32[16]{0:T(128)S(1)} fusion(f32[16,3,3,4096]{3,0,2,1:T(8,128)S(1)} %get-tuple-element.16, f32[4096]{0:T(1024)S(1)} %bitcast.83, f32[16,5,5,4096]{3,0,2,1:T(8,128)S(1)} %pad_convert_fusion, f32[4096]{0:T(1024)S(1)} %bitcast.85, f32[4096]{0:T(1024)S(1)} %bitcast.71, f32[4096]{0:T(1024)S(1)} %bitcast.73, f32[4096]{0:T(1024)S(1)} %bitcast.75, ...), kind=kLoop, calls=%fused_computation.54 | loop fusion | flops 12386288 | bytes 23740480 | tf_op jit(solution)/shard_map/reduce_sum | solution.py:112
  76.2 11.9 %psum.7 = bf16[16]{0:T(256)(128)(2,1)S(1)} all-reduce(f32[16]{0:T(128)S(1)} %multiply_reduce_fusion), channel_id=1, replica_groups=mesh['expert'=8,'chan'=4] {'chan'}, use_global_device_ids=true, to_apply=%region_2.3 | all-reduce | flops 16 | bytes 96 | tf_op jit(solution)/shard_map/psum | solution.py:113
  88.0 0.1 all_to_all.25
  88.1 8.5 %all_to_all.30 = bf16[8,1,2]{2,1,0:T(2,128)(2,1)S(1)} all-to-all(bf16[8,1,2]{2,1,0:T(2,128)(2,1)S(1)} %all_to_all.25), channel_id=1, replica_groups=mesh['expert'=8,'chan'=4] {'expert'}, dimensions={0} | all-to-all | bytes 64 | tf_op jit(solution)/shard_map/all_to_all | solution.py:126
  96.7 3.4 %all-to-all-start.2 = ((bf16[8,2,4608]{2,1,0:T(2,128)(2,1)}), bf16[8,2,4608]{2,1,0:T(2,128)(2,1)S(1)}, u32[]{:S(2)}, u32[]{:S(2)}) async-start(bf16[8,2,4608]{2,1,0:T(2,128)(2,1)} %convert_element_type.194), calls=%async_computation.2 | async-start | bytes 294912 | tf_op jit(solution)/shard_map/all_to_all | solution.py:119
  100.1 0.1 reshape.188
  100.2 0.7 fusion.43
  100.9 4.8 %all-to-all-done.2 = bf16[8,2,4608]{2,1,0:T(2,128)(2,1)S(1)} async-done(((bf16[8,2,4608]{2,1,0:T(2,128)(2,1)}), bf16[8,2,4608]{2,1,0:T(2,128)(2,1)S(1)}, u32[]{:S(2)}, u32[]{:S(2)}) %all-to-all-start.2) | async-done | bytes 147488 | tf_op jit(solution)/shard_map/all_to_all | solution.py:119
  105.7 0.1 reshape.172
  105.7 0.8 convolution_convert_fusion.1
  (20 shorter events, 0.1 us)
Async XLA Ops:
  0.6 1.5 %copy-start = (bf16[8]{0:T(256)(128)(2,1)S(1)}, bf16[8]{0:T(256)(128)(2,1)}, u32[]{:S(2)}) copy-start(bf16[8]{0:T(256)(128)(2,1)} %param.9) | copy-start | bytes 52
  3.0 9.8 %all-to-all-start = ((bf16[8,1,2]{2,1,0:T(2,128)(2,1)}), bf16[8,1,2]{2,1,0:T(2,128)(2,1)S(1)}, u32[]{:S(2)}, u32[]{:S(2)}) async-start(bf16[8,1,2]{2,1,0:T(2,128)(2,1)} %all_to_all.24), calls=%async_computation | async-start | bytes 8192 | tf_op jit(solution)/shard_map/all_to_all | solution.py:87
  12.8 13.6 %all-to-all-start.1 = ((bf16[8,2,9216]{2,1,0:T(2,128)(2,1)}), bf16[8,2,9216]{2,1,0:T(2,128)(2,1)S(1)}, u32[]{:S(2)}, u32[]{:S(2)}) async-start(bf16[8,2,9216]{2,1,0:T(2,128)(2,1)} %reshape.166), calls=%async_computation.1 | async-start | bytes 589824 | tf_op jit(solution)/shard_map/all_to_all | solution.py:80
  57.0 1.7 %copy-start.2 = (f32[3,3,16,2,8,256]{5,4,2,3,1,0:T(8,128)S(1)}, f32[3,3,16,2,8,256]{5,4,2,3,1,0:T(8,128)}, u32[]{:S(2)}) copy-start(f32[3,3,16,2,8,256]{5,4,2,3,1,0:T(8,128)} %copy.35) | copy-start | bytes 7077892
  57.1 1.7 %copy-start.3 = (f32[1,1,4096]{2,1,0:T(1,128)S(1)}, f32[1,1,4096]{2,1,0:T(1,128)}, u32[]{:S(2)}) copy-start(f32[1,1,4096]{2,1,0:T(1,128)} %get-tuple-element.6) | copy-start | bytes 49156
  57.1 1.6 %copy-start.5 = (f32[1,1,4096]{2,1,0:T(1,128)S(1)}, f32[1,1,4096]{2,1,0:T(1,128)}, u32[]{:S(2)}) copy-start(f32[1,1,4096]{2,1,0:T(1,128)} %get-tuple-element.7) | copy-start | bytes 49156
  57.1 1.6 %copy-start.7 = (f32[1,1,4096]{2,1,0:T(1,128)S(1)}, f32[1,1,4096]{2,1,0:T(1,128)}, u32[]{:S(2)}) copy-start(f32[1,1,4096]{2,1,0:T(1,128)} %get-tuple-element.8) | copy-start | bytes 49156
  57.1 1.6 %copy-start.9 = (f32[1,1,4096]{2,1,0:T(1,128)S(1)}, f32[1,1,4096]{2,1,0:T(1,128)}, u32[]{:S(2)}) copy-start(f32[1,1,4096]{2,1,0:T(1,128)} %get-tuple-element.9) | copy-start | bytes 49156
  57.1 1.6 %copy-start.11 = (f32[1,1,4096]{2,1,0:T(1,128)S(1)}, f32[1,1,4096]{2,1,0:T(1,128)}, u32[]{:S(2)}) copy-start(f32[1,1,4096]{2,1,0:T(1,128)} %get-tuple-element.10) | copy-start | bytes 49156
  57.1 1.6 %copy-start.13 = (f32[1,1,4096]{2,1,0:T(1,128)S(1)}, f32[1,1,4096]{2,1,0:T(1,128)}, u32[]{:S(2)}) copy-start(f32[1,1,4096]{2,1,0:T(1,128)} %get-tuple-element.11) | copy-start | bytes 49156
  57.1 1.6 %copy-start.15 = (f32[1,1,4096]{2,1,0:T(1,128)S(1)}, f32[1,1,4096]{2,1,0:T(1,128)}, u32[]{:S(2)}) copy-start(f32[1,1,4096]{2,1,0:T(1,128)} %get-tuple-element.12) | copy-start | bytes 49156
  57.1 1.6 %copy-start.17 = (f32[1,1,4096]{2,1,0:T(1,128)S(1)}, f32[1,1,4096]{2,1,0:T(1,128)}, u32[]{:S(2)}) copy-start(f32[1,1,4096]{2,1,0:T(1,128)} %get-tuple-element.13) | copy-start | bytes 49156
  57.1 1.6 %copy-start.19 = (f32[1,1,4096]{2,1,0:T(1,128)S(1)}, f32[1,1,4096]{2,1,0:T(1,128)}, u32[]{:S(2)}) copy-start(f32[1,1,4096]{2,1,0:T(1,128)} %get-tuple-element.14) | copy-start | bytes 49156
  58.8 7.6 %copy-start.1 = (bf16[3,3,512,256]{3,2,1,0:T(8,128)(2,1)S(1)}, bf16[3,3,512,256]{3,2,1,0:T(8,128)(2,1)}, u32[]{:S(2)}) copy-start(bf16[3,3,512,256]{3,2,1,0:T(8,128)(2,1)} %rev.3) | copy-start | bytes 7077892
  72.4 0.8 copy-start.4
  72.4 0.8 copy-start.6
  72.4 0.8 copy-start.8
  72.4 0.8 copy-start.10
  72.4 0.8 copy-start.12
  72.4 0.8 copy-start.14
  72.4 0.8 copy-start.16
  72.4 0.8 copy-start.18
  72.4 0.8 copy-start.20
  96.7 9.0 %all-to-all-start.2 = ((bf16[8,2,4608]{2,1,0:T(2,128)(2,1)}), bf16[8,2,4608]{2,1,0:T(2,128)(2,1)S(1)}, u32[]{:S(2)}, u32[]{:S(2)}) async-start(bf16[8,2,4608]{2,1,0:T(2,128)(2,1)} %convert_element_type.194), calls=%async_computation.2 | async-start | bytes 294912 | tf_op jit(solution)/shard_map/all_to_all | solution.py:119
where the time goes:
time: 107 us
  blocking collectives  38.2 us (36%)
  matrix products  17.2 us (16%)
  local copies, waits for them, and re-layouts  16.3 us (15%)
  other arithmetic  14.6 us (14%)
  starting transfers between devices  12 us (11%)
  waiting for transfers between devices  7.3 us (7%)
    all_gather x1, blocking collectives, on_device(): gathered = lax.all_gather(grads, 'chan', axis=3, tiled=True)  17.8 us
    psum x1, blocking collectives, on_device(): gate_grad = lax.psum(partial_grad, 'chan').astype(jnp.bfloat16)  11.9 us
    dot_general x1, matrix products, on_device(): lax.dot_general(gathered.reshape(slots * side * side, -1), project, (((1,...  9.3 us
    all_to_all x1, blocking collectives, on_device(): lax.all_to_all(gate_grad.reshape(sections, capacity), 'expert', split_axi...  8.52 us
    convert_element_type x1, other arithmetic, on_device(): active = jax.nn.gelu(h_one, approximate=False).astype(jnp.bfloat16)  7.56 us
    all_to_all x1, starting transfers between devices, on_device(): lax.all_to_all(gate_out.reshape(sections, capacity), 'expert', split_axis...  5.17 us
    all_to_all x1, waiting for transfers between devices, on_device(): lax.all_to_all(d_input.reshape(sections, capacity, -1), 'expert', split_a...  4.82 us
    conv_general_dilated x2, matrix products, group_conv(): lax.conv_general_dilated(field, kernel, (1, 1), 'SAME', dimension_numbers...  4.04 us
  transfers between devices with their start and end apart: 3, of which 2 were waited for; matrix products, arithmetic and copies ran while one was open for 12% of the time, Pallas kernels for 0%

commit v1 on v0

--- a/solution.py
+++ b/solution.py
@@ -1,6 +1,10 @@
+import functools
 import jax
 import jax.numpy as jnp
+import numpy as np
 from jax import lax
+from jax.experimental import pallas as pl
+from jax.experimental.pallas import tpu as pltpu
 from jax.sharding import PartitionSpec as P
 
 CAP = 2
@@ -52,7 +56,7 @@
     return total
 
 
-def on_device(tiles_in, grad_out, gate, expert_id, w_conv, w_depth, w_out):
+def on_device_plain(tiles_in, grad_out, gate, expert_id, w_conv, w_depth, w_out):
     owned, side = (tiles_in.shape[0], tiles_in.shape[1])
     local_feat = tiles_in.shape[3]
     sections = lax.axis_size("expert")
@@ -136,6 +140,555 @@
     return (grad_input.reshape(owned, side, side, local_feat), grad_gate.reshape(owned))
 
 
+LANES = 128
+GROUP_OUT = 256
+MESH = pl.DeviceIdType.MESH
+
+
+def offsets(side):
+    found = []
+    for row in range(-1, 2):
+        for col in range(-1, 2):
+            found.append((row, col))
+    return found
+
+
+def shifted(side, position, row, col):
+    at_row, at_col = position // side + row, position % side + col
+    if 0 <= at_row < side and 0 <= at_col < side:
+        return at_row * side + at_col
+    return None
+
+
+def by_quarter(quarter, parts):
+    shape = next(part for part in parts if part is not None).shape
+    total = None
+    for index, part in enumerate(parts):
+        part = jnp.zeros(shape, jnp.float32) if part is None else part
+        total = part if total is None else jnp.where(quarter == index, part, total)
+    return total
+
+
+def expert_kernel(
+    dims,
+    ids_ref,
+    x_ref,
+    g_ref,
+    base_row_ref,
+    base_col_ref,
+    order_ref,
+    order_back_ref,
+    taps_ref,
+    wc_hbm,
+    wo_hbm,
+    out_ref,
+    wc,
+    wo,
+    zbuf,
+    send,
+    recv,
+    xbuf,
+    gbuf,
+    xcol,
+    h2,
+    slope,
+    upper,
+    dz,
+    gates,
+    wc_sem,
+    wo_sem,
+    zsend_sem,
+    zrecv_sem,
+    send_sem,
+    recv_sem,
+    gsend_sem,
+    grecv_sem,
+):
+    n_e, n_c, owned, tiles_t, side = dims
+    spots = side * side
+    pairs = (spots + 1) // 2
+    slots = n_e * CAP
+    groups = wc.shape[1] // GROUP_OUT
+    per_t = groups // tiles_t
+    width = tiles_t * LANES
+    piece = 2 * CAP * tiles_t
+    me, z = lax.axis_index("expert"), lax.axis_index("chan")
+    offs = offsets(side)
+    taps_used = len(offs)
+
+    order = []
+    for step in range(n_c):
+        block = 0
+        for at in range(n_c):
+            ranked = sorted(range(n_c), key=lambda other: (abs(other - at), other if 2 * at < n_c else -other))
+            block = block + jnp.where(z == at, ranked[step], 0)
+        order.append(block)
+
+    wc_copy = pltpu.make_async_copy(wc_hbm, wc.at[pl.ds(0, wc_hbm.shape[0])], wc_sem)
+    wc_copy.start()
+    wo_copies = []
+    for step in range(n_c):
+        start = pl.multiple_of(order[step] * width, width)
+        wo_copies.append(
+            pltpu.make_async_copy(wo_hbm.at[:, pl.ds(start, width)], wo.at[step], wo_sem.at[step])
+        )
+        wo_copies[step].start()
+
+    barrier = pltpu.get_barrier_semaphore()
+    for step in range(1, n_e):
+        pl.semaphore_signal(
+            barrier, inc=1, device_id=(lax.rem(me + step, n_e), z), device_id_type=MESH
+        )
+    for step in range(1, n_c):
+        pl.semaphore_signal(
+            barrier, inc=1, device_id=(me, lax.rem(z + step, n_c)), device_id_type=MESH
+        )
+
+    names = [ids_ref[tile] for tile in range(owned)]
+    codes = []
+    for tile in range(owned):
+        rank = jnp.int32(0)
+        for earlier in range(tile):
+            rank = rank + jnp.where(names[earlier] == names[tile], 1, 0)
+        codes.append(names[tile] * piece + rank * tiles_t)
+    rows_here, rows_routed = 2 * owned * tiles_t, n_e * piece
+
+    def target(base):
+        total = base & 0xFFFF
+        at_tile = base >> 16
+        for tile in range(owned):
+            total = total + jnp.where(at_tile == tile, codes[tile], 0)
+        return total
+
+    place = jnp.where(
+        lax.broadcasted_iota(jnp.int32, (rows_routed, rows_here), 0) == target(base_row_ref[...]),
+        1.0,
+        0.0,
+    ).astype(jnp.bfloat16)
+
+    def route(block, load):
+        for pair in range(pairs):
+            routed = jnp.dot(place, load(pair), preferred_element_type=jnp.float32)
+            send[block, :, pair] = routed.astype(jnp.bfloat16).reshape(n_e, piece, LANES)
+
+    def exchange(block):
+        copies = []
+        for step in range(1, n_e):
+            peer = lax.rem(me + step, n_e)
+            copies.append(
+                pltpu.make_async_remote_copy(
+                    src_ref=send.at[block, peer],
+                    dst_ref=recv.at[block, me],
+                    send_sem=send_sem.at[block, step],
+                    recv_sem=recv_sem.at[block, step],
+                    device_id=(peer, z),
+                    device_id_type=MESH,
+                )
+            )
+        return copies
+
+    def keep_own(block):
+        recv[block, me] = send[block, me]
+
+    def unroute(block, store):
+        for pair in range(pairs):
+            got = recv[block, :, pair].reshape(rows_routed, LANES)
+            got = jnp.dot(order_ref[...], got, preferred_element_type=jnp.float32)
+            store(pair, got.astype(jnp.bfloat16).reshape(2, tiles_t, slots, LANES))
+
+    def z_copy(source, block, toward):
+        return pltpu.make_async_remote_copy(
+            src_ref=source,
+            dst_ref=zbuf.at[block],
+            send_sem=zsend_sem.at[block, (toward + 1) // 2],
+            recv_sem=zrecv_sem.at[block],
+            device_id=(me, z + toward),
+            device_id_type=MESH,
+        )
+
+    x_block = n_c
+    back_block = n_c + 1
+    route(x_block, lambda pair: x_ref[pair])
+    route(0, lambda pair: g_ref[pair])
+    keep_own(x_block)
+    keep_own(0)
+    pl.semaphore_wait(barrier, n_e - 1 + n_c - 1)
+
+    @pl.when(z > 0)
+    def _():
+        z_copy(g_ref, z, -1).start()
+
+    @pl.when(z < n_c - 1)
+    def _():
+        z_copy(g_ref, z, 1).start()
+
+    all_copies = {}
+    for block in (x_block, 0):
+        all_copies[block] = exchange(block)
+        for copy in all_copies[block]:
+            copy.start()
+
+    def take_z(step):
+        block = order[step]
+        z_copy(zbuf.at[block], block, 1).wait_recv()
+
+        @pl.when((block < z) & (z < n_c - 1))
+        def _():
+            z_copy(zbuf.at[block], block, 1).start()
+
+        @pl.when((block > z) & (z > 0))
+        def _():
+            z_copy(zbuf.at[block], block, -1).start()
+
+        route(step, lambda pair: zbuf[block, pair])
+        keep_own(step)
+        all_copies[step] = exchange(step)
+        for copy in all_copies[step]:
+            copy.start()
+
+    quarter = lax.broadcasted_iota(jnp.int32, (slots, LANES), 1) // (LANES // per_t)
+    half = LANES // per_t
+
+    def forward(tile_t):
+        field = jnp.concatenate([xbuf[tile_t, spot] for spot in range(spots)], axis=0).astype(jnp.float32)
+        turned = [field] + [pltpu.roll(field, half * turn, 1) for turn in range(1, per_t)]
+
+        def part(turn, spot):
+            return None if spot is None else turned[turn][spot * slots : (spot + 1) * slots]
+
+        for inner in range(per_t):
+            for spot in range(spots):
+                for lane_tile in range(wc.shape[0] // LANES):
+                    parts = []
+                    for at in range(per_t):
+                        offset = lane_tile * per_t + at
+                        source = shifted(side, spot, *offs[offset]) if offset < taps_used else None
+                        parts.append(part((at - inner) % per_t, source))
+                    if all(item is None for item in parts):
+                        value = jnp.zeros((slots, LANES), jnp.float32)
+                    else:
+                        value = by_quarter(quarter, parts)
+                    xcol[
+                        inner,
+                        spot * slots : (spot + 1) * slots,
+                        lane_tile * LANES : (lane_tile + 1) * LANES,
+                    ] = value.astype(jnp.bfloat16)
+
+        def each(inner, carry):
+            group = tile_t * per_t + inner
+            lanes = pl.ds(pl.multiple_of(group * GROUP_OUT, GROUP_OUT), GROUP_OUT)
+            h_one = jnp.dot(xcol[inner], wc[:, lanes], preferred_element_type=jnp.float32)
+            for cut in range(GROUP_OUT // LANES):
+                value = h_one[:, cut * LANES : (cut + 1) * LANES]
+                cdf = 0.5 * (1.0 + lax.erf(value * 0.7071067811865476))
+                slant = cdf + value * jnp.exp(-0.5 * value * value) * 0.3989422804014327
+                slope[group, :, cut * LANES : (cut + 1) * LANES] = slant
+                active = (value * cdf).astype(jnp.bfloat16).astype(jnp.float32)
+                taps = taps_ref[group, :, cut * LANES : (cut + 1) * LANES].astype(jnp.float32)
+                for spot in range(spots):
+                    total = None
+                    for index, (row, col) in enumerate(offs):
+                        source = shifted(side, spot, row, col)
+                        if source is not None:
+                            term = active[source * slots : (source + 1) * slots] * taps[index : index + 1]
+                            total = term if total is None else total + term
+                    h2[
+                        group, spot * slots : (spot + 1) * slots, cut * LANES : (cut + 1) * LANES
+                    ] = total.astype(jnp.bfloat16)
+            return carry
+
+        lax.fori_loop(0, per_t, each, 0)
+
+    if n_c > 1:
+        take_z(1)
+    for copy in all_copies[x_block]:
+        copy.wait_recv()
+
+    def store_x(pair, value):
+        for parity in range(2):
+            for tile_t in range(tiles_t):
+                xbuf[tile_t, 2 * pair + parity] = value[parity, tile_t]
+
+    unroute(x_block, store_x)
+    wc[pl.ds(wc_hbm.shape[0], wc.shape[0] - wc_hbm.shape[0])] = jnp.zeros(
+        (wc.shape[0] - wc_hbm.shape[0], wc.shape[1]), jnp.bfloat16
+    )
+    wc_copy.wait()
+    lax.fori_loop(0, tiles_t // 2, lambda at, carry: (forward(at), carry)[1], 0)
+    for step in range(2, min(3, n_c)):
+        take_z(step)
+    lax.fori_loop(tiles_t // 2, tiles_t, lambda at, carry: (forward(at), carry)[1], 0)
+    for step in range(3, n_c):
+        take_z(step)
+
+    gate = xbuf[0, spots].astype(jnp.float32)
+
+    def store_g(pair, value):
+        for parity in range(2):
+            if 2 * pair + parity < spots:
+                for tile_t in range(tiles_t):
+                    gbuf[
+                        (2 * pair + parity) * slots : (2 * pair + parity + 1) * slots,
+                        tile_t * LANES : (tile_t + 1) * LANES,
+                    ] = value[parity, tile_t]
+
+    gates[z] = jnp.zeros((slots, LANES), jnp.float32)
+    for step in range(n_c):
+        for copy in all_copies[step]:
+            copy.wait_recv()
+        unroute(step, store_g)
+        wo_copies[step].wait()
+
+        def each(group, carry):
+            rows = pl.ds(pl.multiple_of(group * GROUP_OUT, GROUP_OUT), GROUP_OUT)
+            product = lax.dot_general(
+                gbuf[...], wo[step, rows], (((1,), (1,)), ((), ())), preferred_element_type=jnp.float32
+            )
+            if step:
+                product = product + upper[group]
+            upper[group] = product
+            if step == n_c - 1:
+                both = product * h2[group].astype(jnp.float32)
+                for spot in range(spots):
+                    for cut in range(GROUP_OUT // LANES):
+                        carry = carry + both[
+                            spot * slots : (spot + 1) * slots, cut * LANES : (cut + 1) * LANES
+                        ]
+            return carry
+
+        summed = lax.fori_loop(0, groups, each, jnp.zeros((slots, LANES), jnp.float32))
+    gates[z] = summed
+    gate_copies = []
+    for step in range(1, n_c):
+        gate_copies.append(
+            pltpu.make_async_remote_copy(
+                src_ref=gates.at[z],
+                dst_ref=gates.at[z],
+                send_sem=gsend_sem.at[step],
+                recv_sem=grecv_sem.at[step],
+                device_id=(me, lax.rem(z + step, n_c)),
+                device_id_type=MESH,
+            )
+        )
+        gate_copies[-1].start()
+
+    def backward(tile_t, carry):
+        folded = []
+        for inner in range(per_t):
+            group = tile_t * per_t + inner
+            lanes = pl.ds(pl.multiple_of(group * GROUP_OUT, GROUP_OUT), GROUP_OUT)
+            sides = []
+            for cut in range(GROUP_OUT // LANES):
+                where = slice(cut * LANES, (cut + 1) * LANES)
+                taps = taps_ref[group, :, where].astype(jnp.float32)
+                d_two = [
+                    (gate * upper[group, spot * slots : (spot + 1) * slots, where])
+                    .astype(jnp.bfloat16)
+                    .astype(jnp.float32)
+                    for spot in range(spots)
+                ]
+                done = []
+                for spot in range(spots):
+                    total = None
+                    for index, (row, col) in enumerate(offs):
+                        source = shifted(side, spot, -row, -col)
+                        if source is not None:
+                            term = d_two[source] * taps[index : index + 1]
+                            total = term if total is None else total + term
+                    slant = slope[group, spot * slots : (spot + 1) * slots, where]
+                    done.append((total * slant).astype(jnp.bfloat16))
+                sides.append(jnp.concatenate(done, axis=0))
+            d_one = jnp.concatenate(sides, axis=1)
+            spread = lax.dot_general(
+                d_one, wc[:, lanes], (((1,), (1,)), ((), ())), preferred_element_type=jnp.float32
+            )
+            sums = []
+            for spot in range(spots):
+                total = None
+                for lane_tile in range(wc.shape[0] // LANES):
+                    parts = []
+                    for at in range(per_t):
+                        offset = lane_tile * per_t + at
+                        source = None
+                        if offset < taps_used:
+                            source = shifted(side, spot, -offs[offset][0], -offs[offset][1])
+                        parts.append(
+                            None
+                            if source is None
+                            else spread[
+                                source * slots : (source + 1) * slots,
+                                lane_tile * LANES : (lane_tile + 1) * LANES,
+                            ]
+                        )
+                    if any(item is not None for item in parts):
+                        value = by_quarter(quarter, parts)
+                        total = value if total is None else total + value
+                sums.append(total)
+            folded.append(sums)
+        for spot in range(spots):
+            total = None
+            for turn in range(per_t):
+                value = by_quarter(
+                    quarter, [folded[(at + turn) % per_t][spot] for at in range(per_t)]
+                )
+                value = pltpu.roll(value, half * turn, 1) if turn else value
+                total = value if total is None else total + value
+            dz[spot, tile_t] = total.astype(jnp.bfloat16)
+        return carry
+
+    lax.fori_loop(0, tiles_t, backward, 0)
+    for copy in gate_copies:
+        copy.wait_recv()
+    total = gates[0]
+    for at in range(1, n_c):
+        total = total + gates[at]
+    total = jnp.broadcast_to(jnp.sum(total, axis=1, keepdims=True), (slots, LANES))
+    for tile_t in range(tiles_t):
+        dz[spots, tile_t] = total.astype(jnp.bfloat16)
+
+    for pair in range(pairs):
+        field = dz[2 * pair : 2 * pair + 2].reshape(rows_routed, LANES)
+        field = jnp.dot(order_back_ref[...], field, preferred_element_type=jnp.float32)
+        send[back_block, :, pair] = field.astype(jnp.bfloat16).reshape(n_e, piece, LANES)
+    all_copies[back_block] = exchange(back_block)
+    for copy in all_copies[back_block]:
+        copy.start()
+    keep_own(back_block)
+    place_back = jnp.where(
+        lax.broadcasted_iota(jnp.int32, (rows_here, rows_routed), 1) == target(base_col_ref[...]),
+        1.0,
+        0.0,
+    ).astype(jnp.bfloat16)
+    for copy in all_copies[back_block]:
+        copy.wait_recv()
+    for pair in range(pairs):
+        got = recv[back_block, :, pair].reshape(rows_routed, LANES)
+        out_ref[pair] = jnp.dot(place_back, got, preferred_element_type=jnp.float32).astype(jnp.bfloat16)
+
+    for block in all_copies:
+        for copy in all_copies[block]:
+            copy.wait_send()
+    for copy in gate_copies:
+        copy.wait_send()
+
+    @pl.when(z > 0)
+    def _():
+        z_copy(g_ref, z, -1).wait_send()
+
+    @pl.when(z < n_c - 1)
+    def _():
+        z_copy(g_ref, z, 1).wait_send()
+
+    for step in range(1, n_c):
+        block = order[step]
+
+        @pl.when((block < z) & (z < n_c - 1))
+        def _():
+            z_copy(zbuf.at[block], block, 1).wait_send()
+
+        @pl.when((block > z) & (z > 0))
+        def _():
+            z_copy(zbuf.at[block], block, -1).wait_send()
+
+
+def on_device(tiles_in, grad_out, gate, expert_id, w_conv, w_depth, w_out):
+    owned, side, local_feat = tiles_in.shape[0], tiles_in.shape[1], tiles_in.shape[3]
+    n_e, n_c = lax.axis_size("expert"), lax.axis_size("chan")
+    hidden = w_out.shape[1]
+    tiles_t = local_feat // LANES
+    spots = side * side
+    pairs = (spots + 1) // 2
+    slots = n_e * CAP
+    piece = 2 * CAP * tiles_t
+    groups = hidden // GROUP_OUT
+    group_in = w_conv.shape[3]
+    rows_here, rows_routed = 2 * owned * tiles_t, n_e * piece
+
+    def by_spot(field, last):
+        field = field.reshape(owned, spots, tiles_t, LANES)
+        last = jnp.broadcast_to(last.reshape(owned, 1, 1, 1), (owned, 1, tiles_t, LANES))
+        field = jnp.concatenate([field, last], axis=1)
+        return field.transpose(1, 0, 2, 3).reshape(pairs, rows_here, LANES)
+
+    x = by_spot(tiles_in, gate)
+    g = by_spot(grad_out, jnp.zeros_like(gate))
+
+    column = np.arange(rows_here)
+    parity, tile, lane_t = column // (owned * tiles_t), column // tiles_t % owned, column % tiles_t
+    base = (tile << 16) + parity * CAP * tiles_t + lane_t
+    base_row = jnp.asarray(base.reshape(1, -1), jnp.int32)
+    base_col = jnp.asarray(base.reshape(-1, 1), jnp.int32)
+    row = np.arange(rows_routed)
+    parity, lane_t = row // (tiles_t * slots), row // slots % tiles_t
+    source, rank = row % slots // CAP, row % CAP
+    order = np.zeros((rows_routed, rows_routed), np.float32)
+    order[row, ((source * 2 + parity) * CAP + rank) * tiles_t + lane_t] = 1.0
+    taps = w_depth[0].reshape(9, groups, GROUP_OUT).transpose(1, 0, 2)
+    taps_rows = 9 * group_in
+    padded_rows = -(-taps_rows // LANES) * LANES
+    dims = (n_e, n_c, owned, tiles_t, side)
+    vmem = pl.BlockSpec(memory_space=pltpu.VMEM)
+    anywhere = pl.BlockSpec(memory_space=pl.ANY)
+    blocks = n_c + 2
+    bf16, f32 = jnp.bfloat16, jnp.float32
+    out = pl.pallas_call(
+        functools.partial(expert_kernel, dims),
+        out_shape=jax.ShapeDtypeStruct((pairs, rows_here, LANES), bf16),
+        in_specs=[pl.BlockSpec(memory_space=pltpu.SMEM)] + [vmem] * 7 + [anywhere] * 2,
+        out_specs=vmem,
+        scratch_shapes=[
+            pltpu.VMEM((padded_rows, hidden), bf16),
+            pltpu.VMEM((n_c, hidden, local_feat), bf16),
+            pltpu.VMEM((n_c, pairs, rows_here, LANES), bf16),
+            pltpu.VMEM((blocks, n_e, pairs, piece, LANES), bf16),
+            pltpu.VMEM((blocks, n_e, pairs, piece, LANES), bf16),
+            pltpu.VMEM((tiles_t, 2 * pairs, slots, LANES), bf16),
+            pltpu.VMEM((spots * slots, local_feat), bf16),
+            pltpu.VMEM((LANES // group_in, spots * slots, padded_rows), bf16),
+            pltpu.VMEM((groups, spots * slots, GROUP_OUT), bf16),
+            pltpu.VMEM((groups, spots * slots, GROUP_OUT), f32),
+            pltpu.VMEM((groups, spots * slots, GROUP_OUT), f32),
+            pltpu.VMEM((2 * pairs, tiles_t, slots, LANES), bf16),
+            pltpu.VMEM((n_c, slots, LANES), f32),
+            pltpu.SemaphoreType.DMA,
+            pltpu.SemaphoreType.DMA((n_c,)),
+            pltpu.SemaphoreType.DMA((n_c, 2)),
+            pltpu.SemaphoreType.DMA((n_c,)),
+            pltpu.SemaphoreType.DMA((blocks, n_e)),
+            pltpu.SemaphoreType.DMA((blocks, n_e)),
+            pltpu.SemaphoreType.DMA((n_c,)),
+            pltpu.SemaphoreType.DMA((n_c,)),
+        ],
+        compiler_params=pltpu.CompilerParams(
+            collective_id=0, has_side_effects=True, vmem_limit_bytes=56 * 1024 * 1024
+        ),
+    )(
+        expert_id.reshape(owned),
+        x,
+        g,
+        base_row,
+        base_col,
+        jnp.asarray(order, bf16),
+        jnp.asarray(order.T, bf16),
+        taps,
+        w_conv.reshape(taps_rows, hidden),
+        w_out.reshape(hidden, w_out.shape[2]),
+    )
+    field = out.reshape(2 * pairs, owned, local_feat)
+    grad_input = field[:spots].transpose(1, 0, 2).reshape(tiles_in.shape)
+    return grad_input, field[spots, :, 0]
+
+
+def choose(tiles_in, grad_out, gate, expert_id, w_conv, w_depth, w_out):
+    owned, side, local_feat = tiles_in.shape[0], tiles_in.shape[1], tiles_in.shape[3]
+    count = local_feat // w_conv.shape[3]
+    whole = local_feat % LANES == 0 and 2 * CAP * (local_feat // LANES) % 16 == 0
+    whole = whole and lax.axis_size("expert") * CAP % 16 == 0 and side % 2 == 1
+    whole = whole and w_out.shape[1] == count * GROUP_OUT and LANES % w_conv.shape[3] == 0
+    body = on_device if whole else on_device_plain
+    return body(tiles_in, grad_out, gate, expert_id, w_conv, w_depth, w_out)
+
+
 def solution(mesh):
     in_specs = (
         P("expert", None, None, "chan"),
@@ -148,5 +701,5 @@
     )
     out_specs = (P("expert", None, None, "chan"), P("expert"))
     return jax.shard_map(
-        on_device, mesh=mesh, in_specs=in_specs, out_specs=out_specs, check_vma=False
+        choose, mesh=mesh, in_specs=in_specs, out_specs=out_specs, check_vma=False
     )

time: 107 us -> 53.6 us (0.50)
  Pallas kernels: 0 us -> 45 us
  blocking collectives: 38.2 us -> 0 us
  matrix products: 17.2 us -> 0 us
  other arithmetic: 14.6 us -> 0.69 us
  starting transfers between devices: 12 us -> 0 us
  local copies, waits for them, and re-layouts: 16.3 us -> 7.01 us
  waiting for transfers between devices: 7.3 us -> 0 us
    pallas_call x0 -> x1, Pallas kernels: none -> 45 us  [on_device(): pl.pallas_call(functools.partial(expert_kernel, dims), out_shape=jax.Shap...]
    all_gather x1 -> x0, blocking collectives: 17.8 us -> none  [on_device(): gathered = lax.all_gather(grads, 'chan', axis=3, tiled=True)]
    dot_general x6 -> x0, matrix products: 13.2 us -> none  [the longest x1 9.3 us: on_device(): lax.dot_general(gathered.reshape(slots * side * side, -1), project, (((1,...]
    all_to_all x3 -> x0, starting transfers between devices: 12 us -> none  [the longest x1 5.17 us: on_device(): lax.all_to_all(gate_out.reshape(sections, capacity), 'expert', split_axis...]
    psum x1 -> x0, blocking collectives: 11.9 us -> none  [on_device(): gate_grad = lax.psum(partial_grad, 'chan').astype(jnp.bfloat16)]
    convert_element_type x5 -> x0, other arithmetic: 11 us -> none  [the longest x1 7.56 us: on_device(): active = jax.nn.gelu(h_one, approximate=False).astype(jnp.bfloat16)]
    all_to_all x1 -> x0, blocking collectives: 8.52 us -> none  [on_device(): lax.all_to_all(gate_grad.reshape(sections, capacity), 'expert', split_axi...]
    all_to_all x3 -> x0, waiting for transfers between devices: 7.3 us -> none  [the longest x1 4.82 us: on_device(): lax.all_to_all(d_input.reshape(sections, capacity, -1), 'expert', split_a...]
  transfers between devices with their start and end apart: 3 -> 0, of which waited for: 2 -> 0; matrix products, arithmetic and copies ran while one was open for 12% -> 0% of each run, Pallas kernels for 0% -> 0%
where the time goes in v1:
time: 53.6 us; the launch traced here: 53.3 us
  Pallas kernels  45 us (84%)
  local copies, waits for them, and re-layouts  7.01 us (13%)
  other arithmetic  0.69 us (1%)
  between operations  0.67 us (1%)
    pallas_call x1, Pallas kernels, on_device(): pl.pallas_call(functools.partial(expert_kernel, dims), out_shape=jax.Shap...  45 us
    reshape x2, local copies, waits for them, and re-layouts, by_spot(): field = field.reshape(owned, spots, tiles_t, LANES)  1.83 us
    unnamed x2, local copies, waits for them, and re-layouts  1.53 us

profile of v1, /device:TPU:0, one launch (start us, length us, event | category | flops | bytes accessed | tf_op | source)
XLA Modules:
  0.0 53.3 jit_solution(14504340599470182968)
XLA Ops:
  0.6 0.7 %broadcast_in_dim.2 = bf16[8,1,4,128]{3,2,0,1:T(4,128)(2,1)S(1)} broadcast(bf16[8]{0:T(256)(128)(2,1)} %param.13), dimensions={0} | broadcast | bytes 8208 | tf_op jit(solution)/shard_map/broadcast_in_dim | solution.py:609
  1.4 0.9 %copy.16 = bf16[8,9,4,128]{3,2,0,1:T(4,128)(2,1)S(1)} copy(bf16[8,9,4,128]{3,0,2,1:T(8,128)(2,1)} %bitcast.29) | data formatting | bytes 147456 | tf_op jit(solution)/shard_map/reshape | solution.py:608
  2.3 0.7 %pad_maximum_fusion = bf16[8,10,4,128]{3,2,0,1:T(4,128)(2,1)} fusion(bf16[8,1,4,128]{3,2,0,1:T(4,128)(2,1)S(1)} %broadcast_in_dim.2, bf16[8,9,4,128]{3,2,0,1:T(4,128)(2,1)S(1)} %copy.16), kind=kLoop, calls=%fused_computation.1 | loop fusion | flops 40960 | bytes 163840 | tf_op jit(solution)/shard_map/concatenate | solution.py:610
  3.0 0.9 %copy.17 = bf16[8,9,4,128]{3,2,0,1:T(4,128)(2,1)S(1)} copy(bf16[8,9,4,128]{3,0,2,1:T(8,128)(2,1)} %bitcast.30) | data formatting | bytes 147456 | tf_op jit(solution)/shard_map/reshape | solution.py:608
  3.9 0.7 %concatenate.7 = bf16[8,10,4,128]{3,2,0,1:T(4,128)(2,1)} pad(bf16[8,9,4,128]{3,2,0,1:T(4,128)(2,1)S(1)} %copy.17, bf16[]{:T(256)} %constant.4.clone.1), padding=0_0x0_1x0_0x0_0 | pad | bytes 155650 | tf_op jit(solution)/shard_map/concatenate | solution.py:610
  4.6 0.9 %copy.21 = bf16[2,8,16,256]{3,2,1,0:T(8,128)(2,1)S(1)} copy(bf16[2,8,16,256]{3,1,2,0:T(8,128)(2,1)} %bitcast.28) | data formatting | bytes 262144
  5.5 0.7 %copy.23 = bf16[9,16,256]{2,0,1:T(8,128)(2,1)} copy(bf16[9,16,256]{2,1,0:T(8,128)(2,1)S(1)} %slice.10) | data formatting | bytes 147456 | tf_op jit(solution)/shard_map/reshape;squeeze | solution.py:626
  6.2 45.0 %shard_map.122 = bf16[5,64,128]{2,1,0:T(8,128)(2,1)} custom-call(s32[8]{0:T(128)} %bitcast.32, bf16[5,64,128]{2,1,0:T(8,128)(2,1)} %bitcast.25, bf16[5,64,128]{2,1,0:T(8,128)(2,1)} %bitcast.26, s32[1,64]{1,0:T(1,128)} %constant.10.clone.base_row_ref, s32[64,1]{1,0:T(8,128)} %constant.11.clone.base_col_ref, bf16[128,128]{1,0:T(8,128)(2,1)} %constant.12.clone.order_ref, ...), custom_call_target="tpu_custom_call" | custom-call | tf_op jit(solution)/shard_map/pallas_call | solution.py:634
  51.1 0.9 %reshape.42 = bf16[10,8,512]{2,1,0:T(8,128)(2,1)S(1)} reshape(bf16[5,64,128]{2,1,0:T(8,128)(2,1)} %shard_map.122) | data formatting | bytes 163840 | tf_op jit(solution)/shard_map/reshape | solution.py:677
  52.1 0.6 %slice.8 = bf16[9,8,512]{2,1,0:T(8,128)(2,1)} slice(bf16[10,8,512]{2,1,0:T(8,128)(2,1)S(1)} %reshape.42), slice={[0:9], [0:8], [0:512]} | slice | bytes 147456 | tf_op jit(solution)/shard_map/slice | solution.py:678
  52.7 0.6 %copy.20 = bf16[1,8,1]{1,2,0:T(2,128)(2,1)} copy(bf16[1,8,1]{2,1,0:T(8,128)(2,1)S(1)} %slice.9) | data formatting | bytes 32
  (2 shorter events, 0.0 us)

commit v2 on v1

--- a/solution.py
+++ b/solution.py
@@ -174,6 +174,7 @@
     ids_ref,
     x_ref,
     g_ref,
+    gate_ref,
     base_row_ref,
     base_col_ref,
     order_ref,
@@ -182,8 +183,10 @@
     wc_hbm,
     wo_hbm,
     out_ref,
+    gate_out_ref,
     wc,
     wo,
+    flat,
     zbuf,
     send,
     recv,
@@ -193,6 +196,8 @@
     h2,
     slope,
     upper,
+    upper_even,
+    upper_odd,
     dz,
     gates,
     wc_sem,
@@ -244,6 +249,10 @@
             barrier, inc=1, device_id=(me, lax.rem(z + step, n_c)), device_id_type=MESH
         )
 
+    wc[pl.ds(wc_hbm.shape[0], wc.shape[0] - wc_hbm.shape[0])] = jnp.zeros(
+        (wc.shape[0] - wc_hbm.shape[0], wc.shape[1]), jnp.bfloat16
+    )
+
     names = [ids_ref[tile] for tile in range(owned)]
     codes = []
     for tile in range(owned):
@@ -266,9 +275,15 @@
         0.0,
     ).astype(jnp.bfloat16)
 
-    def route(block, load):
+    strip = 2 * owned
+
+    def route(block, field):
         for pair in range(pairs):
-            routed = jnp.dot(place, load(pair), preferred_element_type=jnp.float32)
+            taken = field[pair * strip : (pair + 1) * strip, :]
+            taken = jnp.concatenate(
+                [taken[:, at * LANES : (at + 1) * LANES] for at in range(tiles_t)], axis=0
+            )
+            routed = jnp.dot(place, taken, preferred_element_type=jnp.float32)
             send[block, :, pair] = routed.astype(jnp.bfloat16).reshape(n_e, piece, LANES)
 
     def exchange(block):
@@ -296,9 +311,9 @@
             got = jnp.dot(order_ref[...], got, preferred_element_type=jnp.float32)
             store(pair, got.astype(jnp.bfloat16).reshape(2, tiles_t, slots, LANES))
 
-    def z_copy(source, block, toward):
+    def z_copy(block, toward):
         return pltpu.make_async_remote_copy(
-            src_ref=source,
+            src_ref=zbuf.at[block],
             dst_ref=zbuf.at[block],
             send_sem=zsend_sem.at[block, (toward + 1) // 2],
             recv_sem=zrecv_sem.at[block],
@@ -308,48 +323,89 @@
 
     x_block = n_c
     back_block = n_c + 1
-    route(x_block, lambda pair: x_ref[pair])
-    route(0, lambda pair: g_ref[pair])
+    zbuf[z] = jnp.concatenate(
+        [g_ref[...].astype(jnp.float32), jnp.zeros((owned, width), jnp.float32)], axis=0
+    ).astype(jnp.bfloat16)
+    diagonal = lax.broadcasted_iota(jnp.int32, (owned, owned), 0) == lax.broadcasted_iota(
+        jnp.int32, (owned, owned), 1
+    )
+    spread_gate = jnp.where(diagonal, gate_ref[...].astype(jnp.float32), 0.0)
+    spread_gate = jnp.broadcast_to(jnp.sum(spread_gate, axis=1, keepdims=True), (owned, width))
+    flat[...] = jnp.concatenate(
+        [x_ref[...].astype(jnp.float32), spread_gate], axis=0
+    ).astype(jnp.bfloat16)
+    route(x_block, flat)
     keep_own(x_block)
-    keep_own(0)
     pl.semaphore_wait(barrier, n_e - 1 + n_c - 1)
 
     @pl.when(z > 0)
     def _():
-        z_copy(g_ref, z, -1).start()
+        z_copy(z, -1).start()
 
     @pl.when(z < n_c - 1)
     def _():
-        z_copy(g_ref, z, 1).start()
+        z_copy(z, 1).start()
 
     all_copies = {}
-    for block in (x_block, 0):
-        all_copies[block] = exchange(block)
-        for copy in all_copies[block]:
-            copy.start()
+    all_copies[x_block] = exchange(x_block)
+    for copy in all_copies[x_block]:
+        copy.start()
+    route(0, zbuf.at[z])
+    keep_own(0)
+    all_copies[0] = exchange(0)
+    for copy in all_copies[0]:
+        copy.start()
 
     def take_z(step):
         block = order[step]
-        z_copy(zbuf.at[block], block, 1).wait_recv()
+        z_copy(block, 1).wait_recv()
 
         @pl.when((block < z) & (z < n_c - 1))
         def _():
-            z_copy(zbuf.at[block], block, 1).start()
+            z_copy(block, 1).start()
 
         @pl.when((block > z) & (z > 0))
         def _():
-            z_copy(zbuf.at[block], block, -1).start()
-
-        route(step, lambda pair: zbuf[block, pair])
+            z_copy(block, -1).start()
+
+        route(step, zbuf.at[block])
         keep_own(step)
         all_copies[step] = exchange(step)
         for copy in all_copies[step]:
             copy.start()
 
+    def taps_at(group, cut):
+        start = pl.multiple_of(group * GROUP_OUT + cut * LANES, LANES)
+        return taps_ref[:, pl.ds(start, LANES)].astype(jnp.float32)
+
+    def project(step, group):
+        rows = pl.ds(pl.multiple_of(group * GROUP_OUT, GROUP_OUT), GROUP_OUT)
+        return lax.dot_general(
+            gbuf[step], wo[step, rows], (((1,), (1,)), ((), ())), preferred_element_type=jnp.float32
+        )
+
+    def take_block(step):
+        for copy in all_copies[step]:
+            copy.wait_recv()
+
+        def store(pair, value):
+            for parity in range(2):
+                spot = 2 * pair + parity
+                if spot < spots:
+                    for tile_t in range(tiles_t):
+                        gbuf[
+                            step,
+                            spot * slots : (spot + 1) * slots,
+                            tile_t * LANES : (tile_t + 1) * LANES,
+                        ] = value[parity, tile_t]
+
+        unroute(step, store)
+        wo_copies[step].wait()
+
     quarter = lax.broadcasted_iota(jnp.int32, (slots, LANES), 1) // (LANES // per_t)
     half = LANES // per_t
 
-    def forward(tile_t):
+    def forward(tile_t, first, step):
         field = jnp.concatenate([xbuf[tile_t, spot] for spot in range(spots)], axis=0).astype(jnp.float32)
         turned = [field] + [pltpu.roll(field, half * turn, 1) for turn in range(1, per_t)]
 
@@ -378,13 +434,20 @@
             group = tile_t * per_t + inner
             lanes = pl.ds(pl.multiple_of(group * GROUP_OUT, GROUP_OUT), GROUP_OUT)
             h_one = jnp.dot(xcol[inner], wc[:, lanes], preferred_element_type=jnp.float32)
+            if step is not None:
+                for part in range(2):
+                    ahead = 2 * ((tile_t - first) * per_t + inner) + part
+                    if step:
+                        upper[ahead] = upper[ahead] + project(step, ahead)
+                    else:
+                        upper[ahead] = project(step, ahead)
             for cut in range(GROUP_OUT // LANES):
                 value = h_one[:, cut * LANES : (cut + 1) * LANES]
                 cdf = 0.5 * (1.0 + lax.erf(value * 0.7071067811865476))
                 slant = cdf + value * jnp.exp(-0.5 * value * value) * 0.3989422804014327
                 slope[group, :, cut * LANES : (cut + 1) * LANES] = slant
                 active = (value * cdf).astype(jnp.bfloat16).astype(jnp.float32)
-                taps = taps_ref[group, :, cut * LANES : (cut + 1) * LANES].astype(jnp.float32)
+                taps = taps_at(group, cut)
                 for spot in range(spots):
                     total = None
                     for index, (row, col) in enumerate(offs):
@@ -410,69 +473,48 @@
                 xbuf[tile_t, 2 * pair + parity] = value[parity, tile_t]
 
     unroute(x_block, store_x)
-    wc[pl.ds(wc_hbm.shape[0], wc.shape[0] - wc_hbm.shape[0])] = jnp.zeros(
-        (wc.shape[0] - wc_hbm.shape[0], wc.shape[1]), jnp.bfloat16
-    )
     wc_copy.wait()
-    lax.fori_loop(0, tiles_t // 2, lambda at, carry: (forward(at), carry)[1], 0)
-    for step in range(2, min(3, n_c)):
-        take_z(step)
-    lax.fori_loop(tiles_t // 2, tiles_t, lambda at, carry: (forward(at), carry)[1], 0)
-    for step in range(3, n_c):
-        take_z(step)
+    early = min(2, n_c - 1)
+    middle = tiles_t // 2
+    for half_at in range(2):
+        step = half_at if half_at < early else None
+        first, last = (middle, tiles_t) if half_at else (0, middle)
+        if step is not None:
+            take_block(step)
+
+        def walk(tile_t, carry):
+            forward(tile_t, first, step)
+            return carry
+
+        lax.fori_loop(first, last, walk, 0)
+        for at in range(2, n_c):
+            if (at == 2) == (half_at == 0):
+                take_z(at)
+    for step in range(early, n_c):
+        take_block(step)
 
     gate = xbuf[0, spots].astype(jnp.float32)
-
-    def store_g(pair, value):
-        for parity in range(2):
-            if 2 * pair + parity < spots:
-                for tile_t in range(tiles_t):
-                    gbuf[
-                        (2 * pair + parity) * slots : (2 * pair + parity + 1) * slots,
-                        tile_t * LANES : (tile_t + 1) * LANES,
-                    ] = value[parity, tile_t]
-
-    gates[z] = jnp.zeros((slots, LANES), jnp.float32)
-    for step in range(n_c):
-        for copy in all_copies[step]:
-            copy.wait_recv()
-        unroute(step, store_g)
-        wo_copies[step].wait()
-
-        def each(group, carry):
-            rows = pl.ds(pl.multiple_of(group * GROUP_OUT, GROUP_OUT), GROUP_OUT)
-            product = lax.dot_general(
-                gbuf[...], wo[step, rows], (((1,), (1,)), ((), ())), preferred_element_type=jnp.float32
-            )
-            if step:
+    uppers = (upper_even, upper_odd)
+
+    def finish(tile_t, carry):
+        for inner in range(per_t):
+            group = tile_t * per_t + inner
+            product = None
+            for step in range(early, n_c):
+                term = project(step, group)
+                product = term if product is None else product + term
+            if early:
                 product = product + upper[group]
-            upper[group] = product
-            if step == n_c - 1:
-                both = product * h2[group].astype(jnp.float32)
-                for spot in range(spots):
-                    for cut in range(GROUP_OUT // LANES):
-                        carry = carry + both[
-                            spot * slots : (spot + 1) * slots, cut * LANES : (cut + 1) * LANES
-                        ]
-            return carry
-
-        summed = lax.fori_loop(0, groups, each, jnp.zeros((slots, LANES), jnp.float32))
-    gates[z] = summed
-    gate_copies = []
-    for step in range(1, n_c):
-        gate_copies.append(
-            pltpu.make_async_remote_copy(
-                src_ref=gates.at[z],
-                dst_ref=gates.at[z],
-                send_sem=gsend_sem.at[step],
-                recv_sem=grecv_sem.at[step],
-                device_id=(me, lax.rem(z + step, n_c)),
-                device_id_type=MESH,
-            )
-        )
-        gate_copies[-1].start()
-
-    def backward(tile_t, carry):
+            uppers[tile_t % 2][inner] = product
+            both = product * h2[group].astype(jnp.float32)
+            for spot in range(spots):
+                for cut in range(GROUP_OUT // LANES):
+                    carry = carry + both[
+                        spot * slots : (spot + 1) * slots, cut * LANES : (cut + 1) * LANES
+                    ]
+        return carry
+
+    def backward(tile_t):
         folded = []
         for inner in range(per_t):
             group = tile_t * per_t + inner
@@ -480,9 +522,9 @@
             sides = []
             for cut in range(GROUP_OUT // LANES):
                 where = slice(cut * LANES, (cut + 1) * LANES)
-                taps = taps_ref[group, :, where].astype(jnp.float32)
+                taps = taps_at(group, cut)
                 d_two = [
-                    (gate * upper[group, spot * slots : (spot + 1) * slots, where])
+                    (gate * uppers[tile_t % 2][inner, spot * slots : (spot + 1) * slots, where])
                     .astype(jnp.bfloat16)
                     .astype(jnp.float32)
                     for spot in range(spots)
@@ -534,9 +576,27 @@
                 value = pltpu.roll(value, half * turn, 1) if turn else value
                 total = value if total is None else total + value
             dz[spot, tile_t] = total.astype(jnp.bfloat16)
-        return carry
-
-    lax.fori_loop(0, tiles_t, backward, 0)
+
+    summed = finish(0, jnp.zeros((slots, LANES), jnp.float32))
+    for tile_t in range(tiles_t - 1):
+        summed = finish(tile_t + 1, summed)
+        backward(tile_t)
+    gates[z] = summed
+    gate_copies = []
+    for step in range(1, n_c):
+        gate_copies.append(
+            pltpu.make_async_remote_copy(
+                src_ref=gates.at[z],
+                dst_ref=gates.at[z],
+                send_sem=gsend_sem.at[step],
+                recv_sem=grecv_sem.at[step],
+                device_id=(me, lax.rem(z + step, n_c)),
+                device_id_type=MESH,
+            )
+        )
+        gate_copies[-1].start()
+
+    backward(tiles_t - 1)
     for copy in gate_copies:
         copy.wait_recv()
     total = gates[0]
@@ -561,9 +621,19 @@
     ).astype(jnp.bfloat16)
     for copy in all_copies[back_block]:
         copy.wait_recv()
+    back = []
     for pair in range(pairs):
         got = recv[back_block, :, pair].reshape(rows_routed, LANES)
-        out_ref[pair] = jnp.dot(place_back, got, preferred_element_type=jnp.float32).astype(jnp.bfloat16)
+        got = jnp.dot(place_back, got, preferred_element_type=jnp.float32)
+        back.append(
+            jnp.concatenate([got[at * strip : (at + 1) * strip] for at in range(tiles_t)], axis=1)
+        )
+    back = jnp.concatenate(back, axis=0)
+    gate_rows = back[spots * owned :, :owned]
+    gate_out_ref[...] = jnp.sum(
+        jnp.where(diagonal, gate_rows, 0.0), axis=0, keepdims=True
+    ).astype(jnp.bfloat16)
+    out_ref[...] = back[: spots * owned].astype(jnp.bfloat16)
 
     for block in all_copies:
         for copy in all_copies[block]:
@@ -573,22 +643,22 @@
 
     @pl.when(z > 0)
     def _():
-        z_copy(g_ref, z, -1).wait_send()
+        z_copy(z, -1).wait_send()
 
     @pl.when(z < n_c - 1)
     def _():
-        z_copy(g_ref, z, 1).wait_send()
+        z_copy(z, 1).wait_send()
 
     for step in range(1, n_c):
         block = order[step]
 
         @pl.when((block < z) & (z < n_c - 1))
         def _():
-            z_copy(zbuf.at[block], block, 1).wait_send()
+            z_copy(block, 1).wait_send()
 
         @pl.when((block > z) & (z > 0))
         def _():
-            z_copy(zbuf.at[block], block, -1).wait_send()
+            z_copy(block, -1).wait_send()
 
 
 def on_device(tiles_in, grad_out, gate, expert_id, w_conv, w_depth, w_out):
@@ -604,17 +674,8 @@
     group_in = w_conv.shape[3]
     rows_here, rows_routed = 2 * owned * tiles_t, n_e * piece
 
-    def by_spot(field, last):
-        field = field.reshape(owned, spots, tiles_t, LANES)
-        last = jnp.broadcast_to(last.reshape(owned, 1, 1, 1), (owned, 1, tiles_t, LANES))
-        field = jnp.concatenate([field, last], axis=1)
-        return field.transpose(1, 0, 2, 3).reshape(pairs, rows_here, LANES)
-
-    x = by_spot(tiles_in, gate)
-    g = by_spot(grad_out, jnp.zeros_like(gate))
-
     column = np.arange(rows_here)
-    parity, tile, lane_t = column // (owned * tiles_t), column // tiles_t % owned, column % tiles_t
+    lane_t, parity, tile = column // (2 * owned), column // owned % 2, column % owned
     base = (tile << 16) + parity * CAP * tiles_t + lane_t
     base_row = jnp.asarray(base.reshape(1, -1), jnp.int32)
     base_col = jnp.asarray(base.reshape(-1, 1), jnp.int32)
@@ -623,7 +684,6 @@
     source, rank = row % slots // CAP, row % CAP
     order = np.zeros((rows_routed, rows_routed), np.float32)
     order[row, ((source * 2 + parity) * CAP + rank) * tiles_t + lane_t] = 1.0
-    taps = w_depth[0].reshape(9, groups, GROUP_OUT).transpose(1, 0, 2)
     taps_rows = 9 * group_in
     padded_rows = -(-taps_rows // LANES) * LANES
     dims = (n_e, n_c, owned, tiles_t, side)
@@ -631,23 +691,29 @@
     anywhere = pl.BlockSpec(memory_space=pl.ANY)
     blocks = n_c + 2
     bf16, f32 = jnp.bfloat16, jnp.float32
-    out = pl.pallas_call(
+    grad_input, grad_gate = pl.pallas_call(
         functools.partial(expert_kernel, dims),
-        out_shape=jax.ShapeDtypeStruct((pairs, rows_here, LANES), bf16),
-        in_specs=[pl.BlockSpec(memory_space=pltpu.SMEM)] + [vmem] * 7 + [anywhere] * 2,
-        out_specs=vmem,
+        out_shape=(
+            jax.ShapeDtypeStruct((spots * owned, local_feat), bf16),
+            jax.ShapeDtypeStruct((1, owned), bf16),
+        ),
+        in_specs=[pl.BlockSpec(memory_space=pltpu.SMEM)] + [vmem] * 8 + [anywhere] * 2,
+        out_specs=(vmem, vmem),
         scratch_shapes=[
             pltpu.VMEM((padded_rows, hidden), bf16),
             pltpu.VMEM((n_c, hidden, local_feat), bf16),
-            pltpu.VMEM((n_c, pairs, rows_here, LANES), bf16),
+            pltpu.VMEM((2 * pairs * owned, local_feat), bf16),
+            pltpu.VMEM((n_c, 2 * pairs * owned, local_feat), bf16),
             pltpu.VMEM((blocks, n_e, pairs, piece, LANES), bf16),
             pltpu.VMEM((blocks, n_e, pairs, piece, LANES), bf16),
             pltpu.VMEM((tiles_t, 2 * pairs, slots, LANES), bf16),
-            pltpu.VMEM((spots * slots, local_feat), bf16),
+            pltpu.VMEM((n_c, spots * slots, local_feat), bf16),
             pltpu.VMEM((LANES // group_in, spots * slots, padded_rows), bf16),
             pltpu.VMEM((groups, spots * slots, GROUP_OUT), bf16),
             pltpu.VMEM((groups, spots * slots, GROUP_OUT), f32),
             pltpu.VMEM((groups, spots * slots, GROUP_OUT), f32),
+            pltpu.VMEM((groups // tiles_t, spots * slots, GROUP_OUT), f32),
+            pltpu.VMEM((groups // tiles_t, spots * slots, GROUP_OUT), f32),
             pltpu.VMEM((2 * pairs, tiles_t, slots, LANES), bf16),
             pltpu.VMEM((n_c, slots, LANES), f32),
             pltpu.SemaphoreType.DMA,
@@ -664,26 +730,26 @@
         ),
     )(
         expert_id.reshape(owned),
-        x,
-        g,
+        tiles_in.transpose(1, 2, 0, 3).reshape(spots * owned, local_feat),
+        grad_out.transpose(1, 2, 0, 3).reshape(spots * owned, local_feat),
+        gate.reshape(1, owned),
         base_row,
         base_col,
         jnp.asarray(order, bf16),
         jnp.asarray(order.T, bf16),
-        taps,
+        w_depth.reshape(9, hidden),
         w_conv.reshape(taps_rows, hidden),
         w_out.reshape(hidden, w_out.shape[2]),
     )
-    field = out.reshape(2 * pairs, owned, local_feat)
-    grad_input = field[:spots].transpose(1, 0, 2).reshape(tiles_in.shape)
-    return grad_input, field[spots, :, 0]
+    grad_input = grad_input.reshape(side, side, owned, local_feat).transpose(2, 0, 1, 3)
+    return grad_input, grad_gate.reshape(owned)
 
 
 def choose(tiles_in, grad_out, gate, expert_id, w_conv, w_depth, w_out):
     owned, side, local_feat = tiles_in.shape[0], tiles_in.shape[1], tiles_in.shape[3]
     count = local_feat // w_conv.shape[3]
     whole = local_feat % LANES == 0 and 2 * CAP * (local_feat // LANES) % 16 == 0
-    whole = whole and lax.axis_size("expert") * CAP % 16 == 0 and side % 2 == 1
+    whole = whole and lax.axis_size("expert") * CAP % 16 == 0 and side % 2 == 1 and owned % 8 == 0
     whole = whole and w_out.shape[1] == count * GROUP_OUT and LANES % w_conv.shape[3] == 0
     body = on_device if whole else on_device_plain
     return body(tiles_in, grad_out, gate, expert_id, w_conv, w_depth, w_out)

time: 53.6 us -> 42.7 us (0.80)
  Pallas kernels: 45 us -> 39.2 us
  local copies, waits for them, and re-layouts: 7.01 us -> 2.63 us
  other arithmetic: 0.69 us -> 0 us
    pallas_call x1, Pallas kernels: 45 us -> 39.2 us  [on_device(): pl.pallas_call(functools.partial(expert_kernel, dims), out_shape=(jax.Sha...]
    reshape x3 -> x0, local copies, waits for them, and re-layouts: 2.78 us -> none  [the longest x2 1.83 us: by_spot(): field = field.reshape(owned, spots, tiles_t, LANES)]
    unnamed x2, local copies, waits for them, and re-layouts: 1.53 us -> 2.63 us
    broadcast_in_dim x1 -> x0, local copies, waits for them, and re-layouts: 0.73 us -> none  [by_spot(): jnp.broadcast_to(last.reshape(owned, 1, 1, 1), (owned, 1, tiles_t, LANES))]
    concatenate x1 -> x0, other arithmetic: 0.69 us -> none  [by_spot(): field = jnp.concatenate([field, last], axis=1)]
    another operation x2 -> x0, local copies, waits for them, and re-layouts: 0.67 us -> none  [on_device(): taps = w_depth[0].reshape(9, groups, GROUP_OUT).transpose(1, 0, 2)]
    concatenate x1 -> x0, local copies, waits for them, and re-layouts: 0.67 us -> none  [by_spot(): field = jnp.concatenate([field, last], axis=1)]
    slice x2 -> x0, local copies, waits for them, and re-layouts: 0.64 us -> none  [the longest x1 0.64 us: on_device(): grad_input = field[:spots].transpose(1, 0, 2).reshape(tiles_in.shape)]
where the time goes in v2:
time: 42.7 us; the launch traced here: 42.5 us
  Pallas kernels  39.2 us (92%)
  local copies, waits for them, and re-layouts  2.63 us (6%)
  between operations  0.64 us (1%)
    pallas_call x1, Pallas kernels, on_device(): pl.pallas_call(functools.partial(expert_kernel, dims), out_shape=(jax.Sha...  39.2 us
    unnamed x2, local copies, waits for them, and re-layouts  2.63 us

profile of v2, /device:TPU:0, one launch (start us, length us, event | category | flops | bytes accessed | tf_op | source)
XLA Modules:
  0.0 42.5 jit_solution(2744914955734321563)
XLA Ops:
  0.6 39.2 %shard_map.122 = (bf16[72,512]{1,0:T(8,128)(2,1)}, bf16[1,8]{1,0:T(2,128)(2,1)}) custom-call(s32[8]{0:T(128)} %bitcast.21, bf16[72,512]{1,0:T(8,128)(2,1)} %bitcast.18, bf16[72,512]{1,0:T(8,128)(2,1)} %bitcast.19, bf16[1,8]{1,0:T(2,128)(2,1)} %bitcast.22, s32[1,64]{1,0:T(1,128)} %constant.8.clone.base_row_ref, s32[64,1]{1,0:T(8,128)} %constant.9.clone.base_col_ref, ...), custom_call_target="tpu_custom_call" | custom-call | tf_op jit(solution)/shard_map/pallas_call | solution.py:694
  39.8 1.5 %copy.15 = bf16[8,3,3,512]{3,0,2,1:T(8,128)(2,1)} copy(bf16[8,3,3,512]{3,0,2,1:T(8,128)(2,1)} %bitcast.20) | data formatting | bytes 147456
  41.4 1.1 %copy.16 = bf16[8]{0:T(256)(128)(2,1)} copy(bf16[8]{0:T(256)(128)(2,1)} %bitcast.23) | data formatting | bytes 32

commit v3 on v2

--- a/solution.py
+++ b/solution.py
@@ -169,6 +169,55 @@
     return total
 
 
+def slot_codes(ids_ref, owned, piece, tiles_t):
+    names = [ids_ref[tile] for tile in range(owned)]
+    codes = []
+    for tile in range(owned):
+        rank = jnp.int32(0)
+        for earlier in range(tile):
+            rank = rank + jnp.where(names[earlier] == names[tile], 1, 0)
+        codes.append(names[tile] * piece + rank * tiles_t)
+    return codes
+
+
+def target(base, codes):
+    total = base & 0xFFFF
+    at_tile = base >> 16
+    for tile, code in enumerate(codes):
+        total = total + jnp.where(at_tile == tile, code, 0)
+    return total
+
+
+def owner_kernel(dims, ids_ref, base_col_ref, back_ref, out_ref, gate_out_ref):
+    n_e, n_c, owned, tiles_t, side = dims
+    spots = side * side
+    pairs = (spots + 1) // 2
+    piece = 2 * CAP * tiles_t
+    strip = 2 * owned
+    rows_here, rows_routed = 2 * owned * tiles_t, n_e * piece
+    codes = slot_codes(ids_ref, owned, piece, tiles_t)
+    place_back = jnp.where(
+        lax.broadcasted_iota(jnp.int32, (rows_here, rows_routed), 1)
+        == target(base_col_ref[...], codes),
+        1.0,
+        0.0,
+    ).astype(jnp.bfloat16)
+    for pair in range(pairs):
+        got = back_ref[:, pair].reshape(rows_routed, LANES)
+        got = jnp.dot(place_back, got, preferred_element_type=jnp.float32)
+        got = jnp.concatenate([got[at * strip : (at + 1) * strip] for at in range(tiles_t)], axis=1)
+        if pair < pairs - 1:
+            out_ref[pair * strip : (pair + 1) * strip] = got.astype(jnp.bfloat16)
+        else:
+            out_ref[pair * strip :] = got[:owned].astype(jnp.bfloat16)
+            rows = got[owned:, :owned]
+    diagonal = lax.broadcasted_iota(jnp.int32, (owned, owned), 0) == lax.broadcasted_iota(
+        jnp.int32, (owned, owned), 1
+    )
+    gate_row = jnp.sum(jnp.where(diagonal, rows, 0.0), axis=0, keepdims=True)
+    gate_out_ref[...] = gate_row.astype(jnp.bfloat16).reshape(gate_out_ref.shape)
+
+
 def expert_kernel(
     dims,
     ids_ref,
@@ -176,14 +225,12 @@
     g_ref,
     gate_ref,
     base_row_ref,
-    base_col_ref,
     order_ref,
     order_back_ref,
     taps_ref,
     wc_hbm,
     wo_hbm,
-    out_ref,
-    gate_out_ref,
+    back_ref,
     wc,
     wo,
     flat,
@@ -195,7 +242,8 @@
     xcol,
     h2,
     slope,
-    upper,
+    partial_first,
+    partial_second,
     upper_even,
     upper_odd,
     dz,
@@ -208,6 +256,7 @@
     recv_sem,
     gsend_sem,
     grecv_sem,
+    own_sem,
 ):
     n_e, n_c, owned, tiles_t, side = dims
     spots = side * side
@@ -218,6 +267,7 @@
     width = tiles_t * LANES
     piece = 2 * CAP * tiles_t
     me, z = lax.axis_index("expert"), lax.axis_index("chan")
+    partial = (partial_first, partial_second)
     offs = offsets(side)
     taps_used = len(offs)
 
@@ -253,24 +303,11 @@
         (wc.shape[0] - wc_hbm.shape[0], wc.shape[1]), jnp.bfloat16
     )
 
-    names = [ids_ref[tile] for tile in range(owned)]
-    codes = []
-    for tile in range(owned):
-        rank = jnp.int32(0)
-        for earlier in range(tile):
-            rank = rank + jnp.where(names[earlier] == names[tile], 1, 0)
-        codes.append(names[tile] * piece + rank * tiles_t)
+    codes = slot_codes(ids_ref, owned, piece, tiles_t)
     rows_here, rows_routed = 2 * owned * tiles_t, n_e * piece
 
-    def target(base):
-        total = base & 0xFFFF
-        at_tile = base >> 16
-        for tile in range(owned):
-            total = total + jnp.where(at_tile == tile, codes[tile], 0)
-        return total
-
     place = jnp.where(
-        lax.broadcasted_iota(jnp.int32, (rows_routed, rows_here), 0) == target(base_row_ref[...]),
+        lax.broadcasted_iota(jnp.int32, (rows_routed, rows_here), 0) == target(base_row_ref[...], codes),
         1.0,
         0.0,
     ).astype(jnp.bfloat16)
@@ -293,7 +330,7 @@
             copies.append(
                 pltpu.make_async_remote_copy(
                     src_ref=send.at[block, peer],
-                    dst_ref=recv.at[block, me],
+                    dst_ref=back_ref.at[me] if block == back_block else recv.at[block, me],
                     send_sem=send_sem.at[block, step],
                     recv_sem=recv_sem.at[block, step],
                     device_id=(peer, z),
@@ -437,10 +474,7 @@
             if step is not None:
                 for part in range(2):
                     ahead = 2 * ((tile_t - first) * per_t + inner) + part
-                    if step:
-                        upper[ahead] = upper[ahead] + project(step, ahead)
-                    else:
-                        upper[ahead] = project(step, ahead)
+                    partial[step][ahead] = project(step, ahead)
             for cut in range(GROUP_OUT // LANES):
                 value = h_one[:, cut * LANES : (cut + 1) * LANES]
                 cdf = 0.5 * (1.0 + lax.erf(value * 0.7071067811865476))
@@ -460,7 +494,8 @@
                     ] = total.astype(jnp.bfloat16)
             return carry
 
-        lax.fori_loop(0, per_t, each, 0)
+        for inner in range(per_t):
+            each(inner, 0)
 
     if n_c > 1:
         take_z(1)
@@ -486,10 +521,14 @@
             forward(tile_t, first, step)
             return carry
 
-        lax.fori_loop(first, last, walk, 0)
-        for at in range(2, n_c):
-            if (at == 2) == (half_at == 0):
-                take_z(at)
+        if half_at:
+            lax.fori_loop(first, last, walk, 0)
+        else:
+            for tile_t in range(first, last):
+                walk(tile_t, 0)
+                for at in range(2, n_c):
+                    if at - 2 == tile_t or (tile_t == last - 1 and at - 2 > tile_t):
+                        take_z(at)
     for step in range(early, n_c):
         take_block(step)
 
@@ -503,8 +542,8 @@
             for step in range(early, n_c):
                 term = project(step, group)
                 product = term if product is None else product + term
-            if early:
-                product = product + upper[group]
+            for step in range(early):
+                product = product + partial[step][group]
             uppers[tile_t % 2][inner] = product
             both = product * h2[group].astype(jnp.float32)
             for spot in range(spots):
@@ -613,27 +652,11 @@
     all_copies[back_block] = exchange(back_block)
     for copy in all_copies[back_block]:
         copy.start()
-    keep_own(back_block)
-    place_back = jnp.where(
-        lax.broadcasted_iota(jnp.int32, (rows_here, rows_routed), 1) == target(base_col_ref[...]),
-        1.0,
-        0.0,
-    ).astype(jnp.bfloat16)
+    own_copy = pltpu.make_async_copy(send.at[back_block, me], back_ref.at[me], own_sem)
+    own_copy.start()
     for copy in all_copies[back_block]:
         copy.wait_recv()
-    back = []
-    for pair in range(pairs):
-        got = recv[back_block, :, pair].reshape(rows_routed, LANES)
-        got = jnp.dot(place_back, got, preferred_element_type=jnp.float32)
-        back.append(
-            jnp.concatenate([got[at * strip : (at + 1) * strip] for at in range(tiles_t)], axis=1)
-        )
-    back = jnp.concatenate(back, axis=0)
-    gate_rows = back[spots * owned :, :owned]
-    gate_out_ref[...] = jnp.sum(
-        jnp.where(diagonal, gate_rows, 0.0), axis=0, keepdims=True
-    ).astype(jnp.bfloat16)
-    out_ref[...] = back[: spots * owned].astype(jnp.bfloat16)
+    own_copy.wait()
 
     for block in all_copies:
         for copy in all_copies[block]:
@@ -691,25 +714,24 @@
     anywhere = pl.BlockSpec(memory_space=pl.ANY)
     blocks = n_c + 2
     bf16, f32 = jnp.bfloat16, jnp.float32
-    grad_input, grad_gate = pl.pallas_call(
+    ids = expert_id.reshape(owned)
+    back = pl.pallas_call(
         functools.partial(expert_kernel, dims),
-        out_shape=(
-            jax.ShapeDtypeStruct((spots * owned, local_feat), bf16),
-            jax.ShapeDtypeStruct((1, owned), bf16),
-        ),
-        in_specs=[pl.BlockSpec(memory_space=pltpu.SMEM)] + [vmem] * 8 + [anywhere] * 2,
-        out_specs=(vmem, vmem),
+        out_shape=jax.ShapeDtypeStruct((n_e, pairs, piece, LANES), bf16),
+        in_specs=[pl.BlockSpec(memory_space=pltpu.SMEM)] + [vmem] * 7 + [anywhere] * 2,
+        out_specs=anywhere,
         scratch_shapes=[
             pltpu.VMEM((padded_rows, hidden), bf16),
             pltpu.VMEM((n_c, hidden, local_feat), bf16),
             pltpu.VMEM((2 * pairs * owned, local_feat), bf16),
             pltpu.VMEM((n_c, 2 * pairs * owned, local_feat), bf16),
             pltpu.VMEM((blocks, n_e, pairs, piece, LANES), bf16),
-            pltpu.VMEM((blocks, n_e, pairs, piece, LANES), bf16),
+            pltpu.VMEM((blocks - 1, n_e, pairs, piece, LANES), bf16),
             pltpu.VMEM((tiles_t, 2 * pairs, slots, LANES), bf16),
             pltpu.VMEM((n_c, spots * slots, local_feat), bf16),
             pltpu.VMEM((LANES // group_in, spots * slots, padded_rows), bf16),
             pltpu.VMEM((groups, spots * slots, GROUP_OUT), bf16),
+            pltpu.VMEM((groups, spots * slots, GROUP_OUT), f32),
             pltpu.VMEM((groups, spots * slots, GROUP_OUT), f32),
             pltpu.VMEM((groups, spots * slots, GROUP_OUT), f32),
             pltpu.VMEM((groups // tiles_t, spots * slots, GROUP_OUT), f32),
@@ -724,25 +746,34 @@
             pltpu.SemaphoreType.DMA((blocks, n_e)),
             pltpu.SemaphoreType.DMA((n_c,)),
             pltpu.SemaphoreType.DMA((n_c,)),
+            pltpu.SemaphoreType.DMA,
         ],
         compiler_params=pltpu.CompilerParams(
             collective_id=0, has_side_effects=True, vmem_limit_bytes=56 * 1024 * 1024
         ),
     )(
-        expert_id.reshape(owned),
+        ids,
         tiles_in.transpose(1, 2, 0, 3).reshape(spots * owned, local_feat),
         grad_out.transpose(1, 2, 0, 3).reshape(spots * owned, local_feat),
         gate.reshape(1, owned),
         base_row,
-        base_col,
         jnp.asarray(order, bf16),
         jnp.asarray(order.T, bf16),
         w_depth.reshape(9, hidden),
         w_conv.reshape(taps_rows, hidden),
         w_out.reshape(hidden, w_out.shape[2]),
     )
+    grad_input, grad_gate = pl.pallas_call(
+        functools.partial(owner_kernel, dims),
+        out_shape=(
+            jax.ShapeDtypeStruct((spots * owned, local_feat), bf16),
+            jax.ShapeDtypeStruct((owned,), bf16),
+        ),
+        in_specs=[pl.BlockSpec(memory_space=pltpu.SMEM), vmem, vmem],
+        out_specs=(vmem, vmem),
+    )(ids, base_col, back)
     grad_input = grad_input.reshape(side, side, owned, local_feat).transpose(2, 0, 1, 3)
-    return grad_input, grad_gate.reshape(owned)
+    return grad_input, grad_gate
 
 
 def choose(tiles_in, grad_out, gate, expert_id, w_conv, w_depth, w_out):

time: 42.7 us -> 37.6 us (0.88)
  local copies, waits for them, and re-layouts: 2.63 us -> 0 us
  Pallas kernels: 39.2 us -> 36.8 us
    unnamed x2 -> x0, local copies, waits for them, and re-layouts: 2.63 us -> none
    pallas_call x1 -> x2, Pallas kernels: 39.2 us -> 36.8 us  [the longest x1 34.9 us: on_device(): pl.pallas_call(functools.partial(expert_kernel, dims), out_shape=jax.Shap...]
where the time goes in v3:
time: 37.6 us; the launch traced here: 37.4 us
  Pallas kernels  36.8 us (98%)
  between operations  0.64 us (2%)
    pallas_call x1, Pallas kernels, on_device(): pl.pallas_call(functools.partial(expert_kernel, dims), out_shape=jax.Shap...  34.9 us
    pallas_call x1, Pallas kernels, on_device(): pl.pallas_call(functools.partial(owner_kernel, dims), out_shape=(jax.Shap...  1.86 us

profile of v3, /device:TPU:0, one launch (start us, length us, event | category | flops | bytes accessed | tf_op | source)
XLA Modules:
  0.0 37.4 jit_solution(13485188207750154414)
XLA Ops:
  0.6 34.9 %shard_map.122.back_ref = bf16[8,5,16,128]{3,2,1,0:T(8,128)(2,1)} custom-call(s32[8]{0:T(128)} %bitcast.19, bf16[72,512]{1,0:T(8,128)(2,1)} %bitcast.17, bf16[72,512]{1,0:T(8,128)(2,1)} %bitcast.18, bf16[1,8]{1,0:T(2,128)(2,1)} %bitcast.21, s32[1,64]{1,0:T(1,128)} %constant.8.clone.base_row_ref, bf16[128,128]{1,0:T(8,128)(2,1)} %constant.10.clone.order_ref, ...), custom_call_target="tpu_custom_call" | custom-call | tf_op jit(solution)/shard_map/pallas_call | solution.py:718
  35.6 1.9 %shard_map.123 = (bf16[72,512]{1,0:T(8,128)(2,1)}, bf16[8]{0:T(256)(128)(2,1)}) custom-call(s32[8]{0:T(128)} %bitcast.20, s32[64,1]{1,0:T(8,128)} %constant.9.clone.base_col_ref, bf16[8,5,16,128]{3,2,1,0:T(8,128)(2,1)} %shard_map.122.back_ref), custom_call_target="tpu_custom_call" | custom-call | tf_op jit(solution)/shard_map/pallas_call | solution.py:766

commit v4 on v3

--- a/solution.py
+++ b/solution.py
@@ -167,6 +167,29 @@
         part = jnp.zeros(shape, jnp.float32) if part is None else part
         total = part if total is None else jnp.where(quarter == index, part, total)
     return total
+
+
+def normal_parts(value):
+    bell = jnp.exp(-0.5 * value * value)
+    turn = 1.0 / (1.0 + 0.23164188 * jnp.abs(value))
+    series = 0.5307027145
+    for factor in (-0.7265760135, 0.7107068705, -0.142248368, 0.127414796):
+        series = series * turn + factor
+    tail = series * turn * bell
+    return jnp.where(value < 0.0, tail, 1.0 - tail), bell * 0.3989422804014327
+
+
+def depth_sum(side, field, taps, sign):
+    sums = []
+    for spot in range(side * side):
+        total = None
+        for index, (row, col) in enumerate(offsets(side)):
+            source = shifted(side, spot, sign * row, sign * col)
+            if source is not None:
+                term = field[source] * taps[index]
+                total = term if total is None else total + term
+        sums.append(total)
+    return sums
 
 
 def slot_codes(ids_ref, owned, piece, tiles_t):
@@ -413,7 +436,11 @@
 
     def taps_at(group, cut):
         start = pl.multiple_of(group * GROUP_OUT + cut * LANES, LANES)
-        return taps_ref[:, pl.ds(start, LANES)].astype(jnp.float32)
+        taps = taps_ref[:, pl.ds(start, LANES)].astype(jnp.float32)
+        return [
+            jnp.broadcast_to(taps[index : index + 1], (slots, LANES)).astype(jnp.bfloat16)
+            for index in range(taps_used)
+        ]
 
     def project(step, group):
         rows = pl.ds(pl.multiple_of(group * GROUP_OUT, GROUP_OUT), GROUP_OUT)
@@ -477,21 +504,15 @@
                     partial[step][ahead] = project(step, ahead)
             for cut in range(GROUP_OUT // LANES):
                 value = h_one[:, cut * LANES : (cut + 1) * LANES]
-                cdf = 0.5 * (1.0 + lax.erf(value * 0.7071067811865476))
-                slant = cdf + value * jnp.exp(-0.5 * value * value) * 0.3989422804014327
+                cdf, density = normal_parts(value)
+                slant = cdf + value * density
                 slope[group, :, cut * LANES : (cut + 1) * LANES] = slant
-                active = (value * cdf).astype(jnp.bfloat16).astype(jnp.float32)
-                taps = taps_at(group, cut)
-                for spot in range(spots):
-                    total = None
-                    for index, (row, col) in enumerate(offs):
-                        source = shifted(side, spot, row, col)
-                        if source is not None:
-                            term = active[source * slots : (source + 1) * slots] * taps[index : index + 1]
-                            total = term if total is None else total + term
+                active = (value * cdf).astype(jnp.bfloat16)
+                active = [active[spot * slots : (spot + 1) * slots] for spot in range(spots)]
+                for spot, total in enumerate(depth_sum(side, active, taps_at(group, cut), 1)):
                     h2[
                         group, spot * slots : (spot + 1) * slots, cut * LANES : (cut + 1) * LANES
-                    ] = total.astype(jnp.bfloat16)
+                    ] = total
             return carry
 
         for inner in range(per_t):
@@ -561,23 +582,16 @@
             sides = []
             for cut in range(GROUP_OUT // LANES):
                 where = slice(cut * LANES, (cut + 1) * LANES)
-                taps = taps_at(group, cut)
                 d_two = [
-                    (gate * uppers[tile_t % 2][inner, spot * slots : (spot + 1) * slots, where])
-                    .astype(jnp.bfloat16)
-                    .astype(jnp.float32)
+                    (gate * uppers[tile_t % 2][inner, spot * slots : (spot + 1) * slots, where]).astype(
+                        jnp.bfloat16
+                    )
                     for spot in range(spots)
                 ]
                 done = []
-                for spot in range(spots):
-                    total = None
-                    for index, (row, col) in enumerate(offs):
-                        source = shifted(side, spot, -row, -col)
-                        if source is not None:
-                            term = d_two[source] * taps[index : index + 1]
-                            total = term if total is None else total + term
+                for spot, total in enumerate(depth_sum(side, d_two, taps_at(group, cut), -1)):
                     slant = slope[group, spot * slots : (spot + 1) * slots, where]
-                    done.append((total * slant).astype(jnp.bfloat16))
+                    done.append((total.astype(jnp.float32) * slant).astype(jnp.bfloat16))
                 sides.append(jnp.concatenate(done, axis=0))
             d_one = jnp.concatenate(sides, axis=1)
             spread = lax.dot_general(

time: 37.6 us -> 37.4 us (level)
  no operation moved by 1% of the time
where the time goes in v4:
time: 37.4 us; the launch traced here: 37.3 us
  Pallas kernels  36.6 us (98%)
  between operations  0.64 us (2%)
    pallas_call x1, Pallas kernels, on_device(): pl.pallas_call(functools.partial(expert_kernel, dims), out_shape=jax.Shap...  34.8 us
    pallas_call x1, Pallas kernels, on_device(): pl.pallas_call(functools.partial(owner_kernel, dims), out_shape=(jax.Shap...  1.86 us

profile of v4, /device:TPU:0, one launch (start us, length us, event | category | flops | bytes accessed | tf_op | source)
XLA Modules:
  0.0 37.3 jit_solution(6600719897935613365)
XLA Ops:
  0.6 34.8 %shard_map.122.back_ref = bf16[8,5,16,128]{3,2,1,0:T(8,128)(2,1)} custom-call(s32[8]{0:T(128)} %bitcast.19, bf16[72,512]{1,0:T(8,128)(2,1)} %bitcast.17, bf16[72,512]{1,0:T(8,128)(2,1)} %bitcast.18, bf16[1,8]{1,0:T(2,128)(2,1)} %bitcast.21, s32[1,64]{1,0:T(1,128)} %constant.8.clone.base_row_ref, bf16[128,128]{1,0:T(8,128)(2,1)} %constant.10.clone.order_ref, ...), custom_call_target="tpu_custom_call" | custom-call | tf_op jit(solution)/shard_map/pallas_call | solution.py:732
  35.4 1.9 %shard_map.123 = (bf16[72,512]{1,0:T(8,128)(2,1)}, bf16[8]{0:T(256)(128)(2,1)}) custom-call(s32[8]{0:T(128)} %bitcast.20, s32[64,1]{1,0:T(8,128)} %constant.9.clone.base_col_ref, bf16[8,5,16,128]{3,2,1,0:T(8,128)(2,1)} %shard_map.122.back_ref), custom_call_target="tpu_custom_call" | custom-call | tf_op jit(solution)/shard_map/pallas_call | solution.py:780

commit v5 on v3

--- a/solution.py
+++ b/solution.py
@@ -244,6 +244,7 @@
     slope,
     partial_first,
     partial_second,
+    partial_third,
     upper_even,
     upper_odd,
     dz,
@@ -267,7 +268,7 @@
     width = tiles_t * LANES
     piece = 2 * CAP * tiles_t
     me, z = lax.axis_index("expert"), lax.axis_index("chan")
-    partial = (partial_first, partial_second)
+    partial = (partial_first, partial_second, partial_third)
     offs = offsets(side)
     taps_used = len(offs)
 
@@ -442,7 +443,7 @@
     quarter = lax.broadcasted_iota(jnp.int32, (slots, LANES), 1) // (LANES // per_t)
     half = LANES // per_t
 
-    def forward(tile_t, first, step):
+    def forward(tile_t, step):
         field = jnp.concatenate([xbuf[tile_t, spot] for spot in range(spots)], axis=0).astype(jnp.float32)
         turned = [field] + [pltpu.roll(field, half * turn, 1) for turn in range(1, per_t)]
 
@@ -472,8 +473,8 @@
             lanes = pl.ds(pl.multiple_of(group * GROUP_OUT, GROUP_OUT), GROUP_OUT)
             h_one = jnp.dot(xcol[inner], wc[:, lanes], preferred_element_type=jnp.float32)
             if step is not None:
-                for part in range(2):
-                    ahead = 2 * ((tile_t - first) * per_t + inner) + part
+                for part in range(tiles_t):
+                    ahead = inner * tiles_t + part
                     partial[step][ahead] = project(step, ahead)
             for cut in range(GROUP_OUT // LANES):
                 value = h_one[:, cut * LANES : (cut + 1) * LANES]
@@ -509,26 +510,15 @@
 
     unroute(x_block, store_x)
     wc_copy.wait()
-    early = min(2, n_c - 1)
-    middle = tiles_t // 2
-    for half_at in range(2):
-        step = half_at if half_at < early else None
-        first, last = (middle, tiles_t) if half_at else (0, middle)
+    early = min(len(partial), n_c - 1, tiles_t - 1)
+    for tile_t in range(tiles_t):
+        step = tile_t - 1 if 0 < tile_t <= early else None
         if step is not None:
             take_block(step)
-
-        def walk(tile_t, carry):
-            forward(tile_t, first, step)
-            return carry
-
-        if half_at:
-            lax.fori_loop(first, last, walk, 0)
-        else:
-            for tile_t in range(first, last):
-                walk(tile_t, 0)
-                for at in range(2, n_c):
-                    if at - 2 == tile_t or (tile_t == last - 1 and at - 2 > tile_t):
-                        take_z(at)
+        forward(tile_t, step)
+        for at in range(2, n_c):
+            if at - 2 == tile_t or (tile_t == tiles_t - 1 and at - 2 > tile_t):
+                take_z(at)
     for step in range(early, n_c):
         take_block(step)
 
@@ -734,6 +724,7 @@
             pltpu.VMEM((groups, spots * slots, GROUP_OUT), f32),
             pltpu.VMEM((groups, spots * slots, GROUP_OUT), f32),
             pltpu.VMEM((groups, spots * slots, GROUP_OUT), f32),
+            pltpu.VMEM((groups, spots * slots, GROUP_OUT), f32),
             pltpu.VMEM((groups // tiles_t, spots * slots, GROUP_OUT), f32),
             pltpu.VMEM((groups // tiles_t, spots * slots, GROUP_OUT), f32),
             pltpu.VMEM((2 * pairs, tiles_t, slots, LANES), bf16),

time: 37.6 us -> 35.5 us (0.944)
  Pallas kernels: 36.8 us -> 34.7 us
    pallas_call x1, Pallas kernels: 34.9 us -> 32.9 us  [on_device(): pl.pallas_call(functools.partial(expert_kernel, dims), out_shape=jax.Shap...]
where the time goes in v5:
time: 35.5 us; the launch traced here: 35.4 us
  Pallas kernels  34.7 us (98%)
  between operations  0.64 us (2%)
    pallas_call x1, Pallas kernels, on_device(): pl.pallas_call(functools.partial(expert_kernel, dims), out_shape=jax.Shap...  32.9 us
    pallas_call x1, Pallas kernels, on_device(): pl.pallas_call(functools.partial(owner_kernel, dims), out_shape=(jax.Shap...  1.86 us

profile of v5, /device:TPU:0, one launch (start us, length us, event | category | flops | bytes accessed | tf_op | source)
XLA Modules:
  0.0 35.4 jit_solution(17954409881833264876)
XLA Ops:
  0.6 32.9 %shard_map.122.back_ref = bf16[8,5,16,128]{3,2,1,0:T(8,128)(2,1)} custom-call(s32[8]{0:T(128)} %bitcast.19, bf16[72,512]{1,0:T(8,128)(2,1)} %bitcast.17, bf16[72,512]{1,0:T(8,128)(2,1)} %bitcast.18, bf16[1,8]{1,0:T(2,128)(2,1)} %bitcast.21, s32[1,64]{1,0:T(1,128)} %constant.8.clone.base_row_ref, bf16[128,128]{1,0:T(8,128)(2,1)} %constant.10.clone.order_ref, ...), custom_call_target="tpu_custom_call" | custom-call | tf_op jit(solution)/shard_map/pallas_call | solution.py:708
  33.5 1.9 %shard_map.123 = (bf16[72,512]{1,0:T(8,128)(2,1)}, bf16[8]{0:T(256)(128)(2,1)}) custom-call(s32[8]{0:T(128)} %bitcast.20, s32[64,1]{1,0:T(8,128)} %constant.9.clone.base_col_ref, bf16[8,5,16,128]{3,2,1,0:T(8,128)(2,1)} %shard_map.122.back_ref), custom_call_target="tpu_custom_call" | custom-call | tf_op jit(solution)/shard_map/pallas_call | solution.py:757

commit v6 on v5

--- a/solution.py
+++ b/solution.py
@@ -374,6 +374,8 @@
     ).astype(jnp.bfloat16)
     route(x_block, flat)
     keep_own(x_block)
+    route(0, zbuf.at[z])
+    keep_own(0)
     pl.semaphore_wait(barrier, n_e - 1 + n_c - 1)
 
     @pl.when(z > 0)
@@ -388,8 +390,6 @@
     all_copies[x_block] = exchange(x_block)
     for copy in all_copies[x_block]:
         copy.start()
-    route(0, zbuf.at[z])
-    keep_own(0)
     all_copies[0] = exchange(0)
     for copy in all_copies[0]:
         copy.start()
@@ -407,10 +407,10 @@
             z_copy(block, -1).start()
 
         route(step, zbuf.at[block])
-        keep_own(step)
         all_copies[step] = exchange(step)
         for copy in all_copies[step]:
             copy.start()
+        keep_own(step)
 
     def taps_at(group, cut):
         start = pl.multiple_of(group * GROUP_OUT + cut * LANES, LANES)

time: 35.5 us -> 35.5 us (level)
  no operation moved by 1% of the time
where the time goes in v6:
time: 35.5 us; the launch traced here: 35.4 us
  Pallas kernels  34.7 us (98%)
  between operations  0.64 us (2%)
    pallas_call x1, Pallas kernels, on_device(): pl.pallas_call(functools.partial(expert_kernel, dims), out_shape=jax.Shap...  32.9 us
    pallas_call x1, Pallas kernels, on_device(): pl.pallas_call(functools.partial(owner_kernel, dims), out_shape=(jax.Shap...  1.86 us

profile of v6, /device:TPU:0, one launch (start us, length us, event | category | flops | bytes accessed | tf_op | source)
XLA Modules:
  0.0 35.4 jit_solution(7704290684897125676)
XLA Ops:
  0.6 32.9 %shard_map.122.back_ref = bf16[8,5,16,128]{3,2,1,0:T(8,128)(2,1)} custom-call(s32[8]{0:T(128)} %bitcast.19, bf16[72,512]{1,0:T(8,128)(2,1)} %bitcast.17, bf16[72,512]{1,0:T(8,128)(2,1)} %bitcast.18, bf16[1,8]{1,0:T(2,128)(2,1)} %bitcast.21, s32[1,64]{1,0:T(1,128)} %constant.8.clone.base_row_ref, bf16[128,128]{1,0:T(8,128)(2,1)} %constant.10.clone.order_ref, ...), custom_call_target="tpu_custom_call" | custom-call | tf_op jit(solution)/shard_map/pallas_call | solution.py:708
  33.5 1.9 %shard_map.123 = (bf16[72,512]{1,0:T(8,128)(2,1)}, bf16[8]{0:T(256)(128)(2,1)}) custom-call(s32[8]{0:T(128)} %bitcast.20, s32[64,1]{1,0:T(8,128)} %constant.9.clone.base_col_ref, bf16[8,5,16,128]{3,2,1,0:T(8,128)(2,1)} %shard_map.122.back_ref), custom_call_target="tpu_custom_call" | custom-call | tf_op jit(solution)/shard_map/pallas_call | solution.py:757
